TPU v7x, 32 devices: a whole 2x2x4 slice. The times are simulated.
32 devices in a mesh: seq: 8 (over y, x, core), wsh: 4 (over z).
Axes of the slice: x: 2, y: 2, z: 4, core: 2. Of those that a mesh axis runs over, the one named last changes fastest.
Arguments:
- tokens: bfloat16 [4, 8192, 768], P('wsh', 'seq'), may hold values from -6 to 6
- positions: int32 [4, 8192], P('wsh', 'seq'), may hold values from 0 to 8191, as said below
- w_qkv: bfloat16 [768, 2304], P('wsh'), may hold values from -0.21875 to 0.21875
- w_attn: bfloat16 [768, 768], P('wsh'), may hold values from -1.5 to 1.5
- w_in: bfloat16 [768, 2304], P('wsh'), may hold values from -0.21875 to 0.21875
- w_down: bfloat16 [1152, 768], P('wsh'), may hold values from -0.375 to 0.375
- gain_attn: bfloat16 [768], P('wsh'), may hold values from 0.5 to 1.5
- gain_mlp: bfloat16 [768], P('wsh'), may hold values from 0.5 to 1.5
- grad_out: bfloat16 [4, 8192, 768], P('wsh', 'seq'), may hold values from -6 to 6
Outputs:
- mixed: bfloat16 [4, 8192, 768], P('wsh', 'seq')
- grad_tokens: float32 [4, 8192, 768], P('wsh', 'seq')
- grad_qkv: float32 [768, 2304], P('wsh')
- grad_attn: float32 [768, 768], P('wsh')
- grad_in: float32 [768, 2304], P('wsh')
- grad_down: float32 [1152, 768], P('wsh')
- grad_gain_attn: float32 [768], P('wsh')
- grad_gain_mlp: float32 [768], P('wsh')
Inputs may be any that keep to these rules, and one draw needn't show every extreme that they name: In each stream the positions go up by one from token to token inside a sequence and restart at 0 where a new sequence begins. Each stream holds three sequences; the first ends at position 8191, the middle one reaches from the first device of seq to the last.
All inputs are finite; a program needn't handle non-finite values.
Results may differ from a plain program's by a relative error of at most 0.02.
Values may be sent and summed in bfloat16 or wider, within the bound.
A program may use at most 192 MiB of HBM per device.

v0:
```python
import jax
import jax.numpy as jnp
from jax import lax
from jax.sharding import PartitionSpec as P

HEADS = 12
HALF = 64
QBLK = 512


EPS = 1e-05
NEGATIVE = -1e30


def padded(block, sides, width):
    for axis, dim in sides:
        count = lax.axis_size(axis)
        forward = [(i, i + 1) for i in range(count - 1)]
        backward = [(target, source) for source, target in forward]
        low = lax.ppermute(
            lax.slice_in_dim(block, block.shape[dim] - width, None, axis=dim), axis, forward
        )
        high = lax.ppermute(lax.slice_in_dim(block, 0, width, axis=dim), axis, backward)
        block = jnp.concatenate([low, block, high], axis=dim)
    return block


def layer_norm(values, scales):
    centre = jnp.mean(values, axis=-1, keepdims=True)
    shifted = values - centre
    spread = jnp.mean(shifted * shifted, axis=-1, keepdims=True)
    return shifted * lax.rsqrt(spread + EPS) * scales


def rotary(values, places):
    halves = values.shape[-1] // 2
    exponent = jnp.arange(halves, dtype=jnp.float32) * (2.0 / values.shape[-1])
    frequency = jnp.power(jnp.float32(10000.0), -exponent)
    angles = places.astype(jnp.float32)[:, None] * frequency[None, :]
    cosine = jnp.cos(angles)[:, None, :]
    sine = jnp.sin(angles)[:, None, :]
    first = values[..., :halves]
    second = values[..., halves:]
    return jnp.concatenate(
        [first * cosine - second * sine, second * cosine + first * sine], axis=-1
    )


def body(tokens, positions, w_qkv, w_attn, w_in, w_down, gain_attn, gain_mlp, grad_out):
    model_width = w_qkv.shape[1] // 3
    head_count = HEADS
    head_size = model_width // head_count
    hidden_width = w_in.shape[1] // 2
    row_count = tokens.shape[1]
    reach = HALF
    block_rows = QBLK
    span = block_rows + 2 * reach
    block_count = row_count // block_rows
    scale = head_size ** (-0.5)
    gathered = (
        lax.all_gather(w_qkv, "wsh", axis=0, tiled=True),
        lax.all_gather(w_attn, "wsh", axis=0, tiled=True),
        lax.all_gather(w_in, "wsh", axis=0, tiled=True),
        lax.all_gather(w_down, "wsh", axis=0, tiled=True),
        lax.all_gather(gain_attn, "wsh", axis=0, tiled=True),
        lax.all_gather(gain_mlp, "wsh", axis=0, tiled=True),
    )
    full_qkv, full_attn, full_in, full_down, full_gain_a, full_gain_m = gathered
    scales_attn = full_gain_a.astype(jnp.float32)
    scales_mlp = full_gain_m.astype(jnp.float32)
    x_in = tokens[0].astype(jnp.float32)
    places = positions[0]
    places_wide = padded(places, (("seq", 0),), reach)
    stream_start = lax.axis_index("seq") * row_count
    stream_total = lax.axis_size("seq") * row_count
    normed_f, norm_one_pull = jax.vjp(layer_norm, x_in, scales_attn)
    normed_attn = normed_f.astype(jnp.bfloat16)
    qkv = jnp.dot(normed_attn, full_qkv, preferred_element_type=jnp.float32)

    def rotate_pair(query_raw, key_raw):
        return (rotary(query_raw, places), rotary(key_raw, places))

    (rot_query, rot_key), rotary_pull = jax.vjp(
        rotate_pair,
        qkv[:, :model_width].reshape(row_count, head_count, head_size),
        qkv[:, model_width : 2 * model_width].reshape(row_count, head_count, head_size),
    )
    query_low = rot_query.astype(jnp.bfloat16)
    key_low = rot_key.astype(jnp.bfloat16).reshape(row_count, model_width)
    value_low = qkv[:, 2 * model_width :].astype(jnp.bfloat16)
    kv_wide = padded(jnp.concatenate([key_low, value_low], axis=1), (("seq", 0),), reach)

    def allowed_of(offset):
        local_rows = offset + jnp.arange(block_rows, dtype=jnp.int32)
        local_cols = offset - reach + jnp.arange(span, dtype=jnp.int32)
        row_places = places[offset : offset + block_rows]
        col_places = places_wide[offset : offset + span]
        near = jnp.abs(local_rows[:, None] - local_cols[None, :]) <= reach
        global_cols = stream_start + local_cols
        inside = ((global_cols >= 0) & (global_cols < stream_total))[None, :]
        same = (
            col_places[None, :] - row_places[:, None] == local_cols[None, :] - local_rows[:, None]
        )
        return near & inside & same

    def pieces_of(offset):
        query_block = query_low[offset : offset + block_rows]
        kv_block = kv_wide[offset : offset + span]
        key_block = kv_block[:, :model_width].reshape(span, head_count, head_size)
        value_block = kv_block[:, model_width:].reshape(span, head_count, head_size)
        raw = (
            jnp.einsum("qhd,khd->hqk", query_block, key_block, preferred_element_type=jnp.float32)
            * scale
        )
        masked = jnp.where(allowed_of(offset)[None], raw, NEGATIVE)
        return (query_block, key_block, value_block, masked)

    context_parts = []
    log_totals = []
    for block_index in range(block_count):
        offset = block_index * block_rows
        query_block, key_block, value_block, masked = pieces_of(offset)
        peak = jnp.max(masked, axis=-1, keepdims=True)
        raised = jnp.exp(masked - peak)
        totals = jnp.sum(raised, axis=-1, keepdims=True)
        probs = raised / totals
        log_totals.append(peak + jnp.log(totals))
        context_parts.append(
            jnp.einsum(
                "hqk,khd->qhd",
                probs.astype(jnp.bfloat16),
                value_block,
                preferred_element_type=jnp.float32,
            )
        )
    context = (
        jnp.concatenate(context_parts, axis=0).reshape(row_count, model_width).astype(jnp.bfloat16)
    )
    resid = x_in + jnp.dot(context, full_attn, preferred_element_type=jnp.float32)
    normed_m, norm_two_pull = jax.vjp(layer_norm, resid, scales_mlp)
    normed_mlp = normed_m.astype(jnp.bfloat16)
    gate_up = jnp.dot(normed_mlp, full_in, preferred_element_type=jnp.float32)

    def gated(values):
        return jax.nn.gelu(values[:, :hidden_width], approximate=False) * values[:, hidden_width:]

    hidden_f, gated_pull = jax.vjp(gated, gate_up)
    hidden = hidden_f.astype(jnp.bfloat16)
    mixed = (resid + jnp.dot(hidden, full_down, preferred_element_type=jnp.float32)).astype(
        jnp.bfloat16
    )
    cotangent = grad_out[0]
    dy_f = cotangent.astype(jnp.float32)
    grad_down = jnp.einsum("tf,td->fd", hidden, cotangent, preferred_element_type=jnp.float32)
    d_hidden = jnp.einsum("td,fd->tf", cotangent, full_down, preferred_element_type=jnp.float32)
    (d_gate_up,) = gated_pull(d_hidden)
    d_gate_low = d_gate_up.astype(jnp.bfloat16)
    grad_in = jnp.einsum("td,te->de", normed_mlp, d_gate_low, preferred_element_type=jnp.float32)
    d_normed_mlp = jnp.einsum("te,de->td", d_gate_low, full_in, preferred_element_type=jnp.float32)
    d_resid_norm, grad_gain_m = norm_two_pull(d_normed_mlp)
    d_resid = dy_f + d_resid_norm
    d_resid_low = d_resid.astype(jnp.bfloat16)
    grad_attn = jnp.einsum("td,te->de", context, d_resid_low, preferred_element_type=jnp.float32)
    d_context = jnp.einsum("te,de->td", d_resid_low, full_attn, preferred_element_type=jnp.float32)
    d_context_low = d_context.astype(jnp.bfloat16).reshape(row_count, head_count, head_size)
    query_grads = []
    kv_grads = jnp.zeros((row_count + 2 * reach, 2 * model_width), jnp.float32)
    for block_index in range(block_count):
        offset = block_index * block_rows
        query_block, key_block, value_block, masked = pieces_of(offset)
        probs = jnp.exp(masked - log_totals[block_index])
        d_block = d_context_low[offset : offset + block_rows]
        d_probs = jnp.einsum(
            "qhd,khd->hqk", d_block, value_block, preferred_element_type=jnp.float32
        )
        d_values = jnp.einsum(
            "hqk,qhd->khd", probs.astype(jnp.bfloat16), d_block, preferred_element_type=jnp.float32
        )
        d_scores = probs * (d_probs - jnp.sum(d_probs * probs, axis=-1, keepdims=True))
        d_scores_low = d_scores.astype(jnp.bfloat16)
        query_grads.append(
            jnp.einsum("hqk,khd->qhd", d_scores_low, key_block, preferred_element_type=jnp.float32)
            * scale
        )
        d_keys = (
            jnp.einsum(
                "hqk,qhd->khd", d_scores_low, query_block, preferred_element_type=jnp.float32
            )
            * scale
        )
        joined = jnp.concatenate(
            [d_keys.reshape(span, model_width), d_values.reshape(span, model_width)], axis=1
        )
        kv_grads = kv_grads.at[offset : offset + span].add(joined)
    outer_edges = jnp.concatenate([kv_grads[:reach], kv_grads[-reach:]], axis=0)
    returned = padded(outer_edges.astype(jnp.bfloat16), (("seq", 0),), reach).astype(
        outer_edges.dtype
    )
    own_grads = kv_grads[reach : reach + row_count]
    own_grads = own_grads.at[:reach].add(returned[:reach])
    own_grads = own_grads.at[row_count - reach :].add(returned[-reach:])
    d_rot_query = jnp.concatenate(query_grads, axis=0)
    d_rot_key = own_grads[:, :model_width].reshape(row_count, head_count, head_size)
    d_query_raw, d_key_raw = rotary_pull((d_rot_query, d_rot_key))
    d_qkv = jnp.concatenate(
        [
            d_query_raw.reshape(row_count, model_width),
            d_key_raw.reshape(row_count, model_width),
            own_grads[:, model_width:],
        ],
        axis=1,
    ).astype(jnp.bfloat16)
    grad_qkv = jnp.einsum("td,te->de", normed_attn, d_qkv, preferred_element_type=jnp.float32)
    d_normed_attn = jnp.einsum("te,de->td", d_qkv, full_qkv, preferred_element_type=jnp.float32)
    d_input_norm, grad_gain_a = norm_one_pull(d_normed_attn)
    grad_tokens = (d_resid + d_input_norm)[None]
    terms = (grad_qkv, grad_attn, grad_in, grad_down, grad_gain_a, grad_gain_m)
    summed = lax.psum((terms[0], terms[1], terms[2], terms[3], terms[4], terms[5]), "seq")
    shares = (
        lax.psum_scatter(
            summed[0].astype(jnp.bfloat16), "wsh", scatter_dimension=0, tiled=True
        ).astype(jnp.float32),
        lax.psum_scatter(
            summed[1].astype(jnp.bfloat16), "wsh", scatter_dimension=0, tiled=True
        ).astype(jnp.float32),
        lax.psum_scatter(
            summed[2].astype(jnp.bfloat16), "wsh", scatter_dimension=0, tiled=True
        ).astype(jnp.float32),
        lax.psum_scatter(
            summed[3].astype(jnp.bfloat16), "wsh", scatter_dimension=0, tiled=True
        ).astype(jnp.float32),
        lax.psum_scatter(
            summed[4].astype(jnp.bfloat16), "wsh", scatter_dimension=0, tiled=True
        ).astype(jnp.float32),
        lax.psum_scatter(
            summed[5].astype(jnp.bfloat16), "wsh", scatter_dimension=0, tiled=True
        ).astype(jnp.float32),
    )
    return (
        mixed[None],
        grad_tokens,
        shares[0],
        shares[1],
        shares[2],
        shares[3],
        shares[4],
        shares[5],
    )


def solution(mesh):
    return jax.shard_map(
        body,
        mesh=mesh,
        in_specs=(
            P("wsh", "seq", None),
            P("wsh", "seq"),
            P("wsh", None),
            P("wsh", None),
            P("wsh", None),
            P("wsh", None),
            P("wsh"),
            P("wsh"),
            P("wsh", "seq", None),
        ),
        out_specs=(
            P("wsh", "seq", None),
            P("wsh", "seq", None),
            P("wsh", None),
            P("wsh", None),
            P("wsh", None),
            P("wsh", None),
            P("wsh"),
            P("wsh"),
        ),
        check_vma=False,
    )
```

profile of v0, /device:TPU:0, one launch (start us, length us, event | category | flops | bytes accessed | tf_op | source)
XLA Modules:
  0.0 1001.0 jit_solution(15496215242527700388)
XLA Ops:
  18.1 13.2 %all-reduce.13 = (bf16[768]{0:T(1024)(128)(2,1)S(1)}, bf16[768]{0:T(1024)(128)(2,1)S(1)}) all-reduce(bf16[768]{0:T(1024)(128)(2,1)S(1)} %dynamic-update-slice.12, bf16[768]{0:T(1024)(128)(2,1)S(1)} %dynamic-update-slice.13), channel_id=1, replica_groups=mesh['seq'=8,'wsh'=4] {'wsh'}, use_global_device_ids=true, to_apply=%add.7 | all-reduce | flops 1536 | bytes 6144
  33.6 48.9 %all-gather.5.cloned.1.call-done = bf16[768,2304]{1,0:T(8,128)(2,1)} async-done(((bf16[192,2304]{1,0:T(8,128)(2,1)}), bf16[768,2304]{1,0:T(8,128)(2,1)}) %all-gather.5.cloned.1.call-update) | async-done | bytes 3538960 | tf_op jit(solution)/shard_map/all_gather | solution.py:61
  82.5 6.2 fusion.54
  88.7 3.1 fusion.69
  93.1 3.5 copy.48
  96.6 3.6 copy.51
  100.2 3.9 subtract_convert_fusion
  105.6 2.6 copy.49
  115.8 3.4 pad_maximum_fusion.9
  128.2 4.5 fusion.74
  132.7 3.4 fusion
  138.3 5.1 fusion.47
  143.5 3.3 fusion.73
  146.7 3.4 fusion.1
  152.3 5.5 fusion.48
  158.1 3.3 fusion.75
  163.5 20.4 %all-gather.9.cloned.1.call-done = bf16[768,2304]{1,0:T(8,128)(2,1)} async-done(((bf16[192,2304]{1,0:T(8,128)(2,1)}), bf16[768,2304]{1,0:T(8,128)(2,1)}) %all-gather.9.cloned.1.call-update) | async-done | bytes 3538960 | tf_op jit(solution)/shard_map/all_gather | solution.py:63
  184.0 10.5 %fusion.66 = f32[1024,2304]{1,0:T(8,128)} fusion(bf16[768,2304]{1,0:T(8,128)(2,1)} %all-gather.9.cloned.1.call-done, f32[1024,768]{0,1:T(8,128)} %copy-done.15, f32[768]{0:T(1024)S(1)} %convert_element_type.123, f32[1024]{0:T(1024)S(1)} %fusion.57, f32[1024]{0:T(1024)S(1)} %broadcast_multiply_fusion), kind=kOutput, calls=%fused_computation.167 | convolution fusion | flops 3627024384 | bytes 16133120 | tf_op jit(solution)/shard_map/dot_general | solution.py:142
  194.5 29.9 %all-gather.11.cloned.1.call-done = bf16[1152,768]{1,0:T(8,128)(2,1)} async-done(((bf16[288,768]{1,0:T(8,128)(2,1)}), bf16[1152,768]{1,0:T(8,128)(2,1)}) %all-gather.11.cloned.1.call-update) | async-done | bytes 1769488 | tf_op jit(solution)/shard_map/all_gather | solution.py:64
  224.4 14.9 %fusion.39 = (f32[1024,1152]{1,0:T(8,128)}, f32[1024,1152]{1,0:T(8,128)S(1)}, f32[1024,1152]{1,0:T(8,128)S(1)}) fusion(f32[1024,2304]{1,0:T(8,128)} %fusion.66, bf16[1152,768]{1,0:T(8,128)(2,1)} %all-gather.11.cloned.1.call-done, bf16[1,1024,768]{2,1,0:T(8,128)(2,1)S(1)} %copy-done.32), kind=kOutput, calls=%fused_computation.101 | convolution fusion | flops 1888616448 | bytes 22216704 | tf_op jit(solution)/shard_map/td,fd->tf/dot_general | solution.py:155
  239.2 3.7 multiply_add_fusion
  243.0 9.3 fusion.50
  252.3 4.2 multiply_reduce_fusion.2
  262.7 15.1 %multiply_reduce_fusion = (f32[12,512]{1,0:T(8,128)S(1)}, f32[12,512,640]{2,1,0:T(8,128)}) fusion(f32[12,512,640]{2,1,0:T(8,128)} %copy-done.1, f32[12,512]{1,0:T(8,128)S(1)} %log_add_fusion, bf16[512,12,64]{0,2,1:T(8,128)(2,1)S(1)} %bitcast.140, bf16[640,12,64]{0,2,1:T(8,128)(2,1)S(1)} %bitcast.146), kind=kOutput, calls=%fused_computation.1 | convolution fusion | flops 515106816 | bytes 33275904 | tf_op jit(solution)/shard_map/qhd,khd->hqk/dot_general | solution.py:173
  277.8 8.3 fusion.4
  286.2 9.6 multiply_reduce_fusion.1
  295.8 4.1 fusion.6
  300.0 11.6 %multiply_convert_fusion = bf16[12,512,640]{2,1,0:T(8,128)(2,1)S(1)} fusion(f32[12,512,640]{2,1,0:T(8,128)} %get-tuple-element.147, f32[12,512,640]{2,1,0:T(8,128)} %copy-done.1, f32[12,512]{1,0:T(8,128)S(1)} %get-tuple-element.146, f32[12,512]{1,0:T(8,128)S(1)} %log_add_fusion), kind=kLoop, calls=%fused_computation | loop fusion | flops 15728640 | bytes 39370752 | tf_op jit(solution)/shard_map/convert_element_type | solution.py:180
  311.6 3.1 convolution_multiply_fusion
  315.3 7.9 multiply_convert_fusion.1
  328.7 2.8 constant_dynamic-update-slice_fusion
  331.6 4.8 slice.266
  336.4 3.7 multiply_bitcast_fusion
  340.2 3.7 multiply_bitcast_fusion.1
  348.1 4.0 fusion.35
  352.1 2.9 fusion.76
  356.6 5.2 scatter-add.16
  364.2 4.9 scatter-add.19
  377.1 6.8 fusion.32
  383.9 3.9 fusion.30
  390.7 395.6 %all-reduce.15 = (bf16[768,2304]{1,0:T(8,128)(2,1)}, bf16[768,768]{1,0:T(8,128)(2,1)}, bf16[768,2304]{1,0:T(8,128)(2,1)}, bf16[1152,768]{1,0:T(8,128)(2,1)}, bf1...) all-reduce(f32[768,2304]{1,0:T(8,128)} %fusion.32, ...), channel_id=1, replica_groups=mesh['seq'=8,'wsh'=4] {'seq'}, use_global_device_ids=true, to_apply=%region_14.15 | all-reduce | flops 5015040 | bytes 30090240 | tf_op jit(solution)/shard_map/psum | solution.py:218
  789.1 6.8 fusion.40
  798.4 5.9 add_bitcast_fusion
  804.3 3.6 copy.58
  807.9 9.3 all-reduce.12
  820.3 34.1 %reduce-scatter.11.cloned.1.call-done = bf16[288,768]{1,0:T(8,128)(2,1)} async-done(((bf16[1152,768]{1,0:T(8,128)(2,1)}), bf16[288,768]{1,0:T(8,128)(2,1)}) %reduce-scatter.11.cloned.1.call-update) | async-done | bytes 442384 | tf_op jit(solution)/shard_map/reduce_scatter | solution.py:229
  856.4 65.9 %reduce-scatter.5.cloned.1.call-done = bf16[192,2304]{1,0:T(8,128)(2,1)} async-done(((bf16[768,2304]{1,0:T(8,128)(2,1)}), bf16[192,2304]{1,0:T(8,128)(2,1)}) %reduce-scatter.5.cloned.1.call-update) | async-done | bytes 884752 | tf_op jit(solution)/shard_map/reduce_scatter | solution.py:220
  924.8 66.6 %reduce-scatter.9.cloned.1.call-done = bf16[192,2304]{1,0:T(8,128)(2,1)} async-done(((bf16[768,2304]{1,0:T(8,128)(2,1)}), bf16[192,2304]{1,0:T(8,128)(2,1)}) %reduce-scatter.9.cloned.1.call-update) | async-done | bytes 884752 | tf_op jit(solution)/shard_map/reduce_scatter | solution.py:226
  (235 shorter events, 84.6 us)
Async XLA Ops:
  7.2 7.5 copy-start.30
  7.2 75.3 %all-gather.5.cloned.1.call-start = ((), (), s32[]{:S(2)}) async-start(), calls=%async_computation.4 | async-start | bytes 4423680 | tf_op jit(solution)/shard_map/all_gather | solution.py:61
  7.9 150.2 %all-gather.7.cloned.1.call-start = ((), (), s32[]{:S(2)}) async-start(), calls=%async_computation.5 | async-start | bytes 1474560 | tf_op jit(solution)/shard_map/all_gather | solution.py:62
  8.7 175.3 %all-gather.9.cloned.1.call-start = ((), (), s32[]{:S(2)}) async-start(), calls=%async_computation.6 | async-start | bytes 4423680 | tf_op jit(solution)/shard_map/all_gather | solution.py:63
  9.4 215.0 %all-gather.11.cloned.1.call-start = ((), (), s32[]{:S(2)}) async-start(), calls=%async_computation.7 | async-start | bytes 2211840 | tf_op jit(solution)/shard_map/all_gather | solution.py:64
  10.2 23.4 %collective-permute-start.1 = (s32[64]{0:T(128)S(1)}, s32[64]{0:T(128)S(1)}, u32[]{:S(2)}, u32[]{:S(2)}) collective-permute-start(s32[64]{0:T(128)S(1)} %get-tuple-element.130), channel_id=1, source_target_pairs={{0,4},{4,8},{8,12},{12,16},{16,20},{20,24},{24,28},{1,5},{5,9},{9,... | collective-permute-start | bytes 776 | tf_op jit(solution)/shard_map/ppermute | solution.py:20
  12.5 21.0 %collective-permute-start.3 = (s32[64]{0:T(128)S(1)}, s32[64]{0:T(128)S(1)}, u32[]{:S(2)}, u32[]{:S(2)}) collective-permute-start(s32[64]{0:T(128)S(1)} %get-tuple-element.131), channel_id=1, source_target_pairs={{4,0},{8,4},{12,8},{16,12},{20,16},{24,20},{28,24},{5,1},{9,5},{13... | collective-permute-start | bytes 776 | tf_op jit(solution)/shard_map/ppermute | solution.py:23
  13.9 804.6 %reduce-scatter.7.cloned.1.call-start = ((), (), s32[]{:S(2)}) async-start(), calls=%async_computation.9 | async-start | bytes 1474560 | tf_op jit(solution)/shard_map/reduce_scatter | solution.py:223
  15.5 142.6 %copy-start.4 = (bf16[1,1024,768]{1,2,0:T(8,128)(2,1)}, bf16[1,1024,768]{1,2,0:T(8,128)(2,1)S(1)}, u32[]{:S(2)}) copy-start(bf16[1,1024,768]{1,2,0:T(8,128)(2,1)S(1)} %copy.47) | copy-start | bytes 4718596
  15.5 16.3 %copy-start.31 = (bf16[1,1024,768]{2,1,0:T(8,128)(2,1)S(1)}, bf16[1,1024,768]{2,1,0:T(8,128)(2,1)}, u32[]{:S(2)}) copy-start(bf16[1,1024,768]{2,1,0:T(8,128)(2,1)} %param.25) | copy-start | bytes 4718596
  15.8 72.9 %copy-start.44 = (f32[1024]{0:T(1024)}, f32[1024]{0:T(1024)S(1)}, u32[]{:S(2)}) copy-start(f32[1024]{0:T(1024)S(1)} %broadcast_multiply_fusion.1) | copy-start | bytes 12292
  16.3 72.4 %copy-start.47 = (f32[1024]{0:T(1024)}, f32[1024]{0:T(1024)S(1)}, u32[]{:S(2)}) copy-start(f32[1024]{0:T(1024)S(1)} %fusion.56) | copy-start | bytes 12292
  31.8 68.4 %copy-start.38 = (f32[1024,32]{0,1:T(8,128)}, f32[1024,32]{0,1:T(8,128)S(1)}, u32[]{:S(2)}) copy-start(f32[1024,32]{0,1:T(8,128)S(1)} %get-tuple-element.126) | copy-start | bytes 393220
  31.8 68.4 %copy-start.40 = (f32[1024,32]{0,1:T(8,128)}, f32[1024,32]{0,1:T(8,128)S(1)}, u32[]{:S(2)}) copy-start(f32[1024,32]{0,1:T(8,128)S(1)} %get-tuple-element.127) | copy-start | bytes 393220
  31.8 56.9 %copy-start.49 = (f32[768]{0:T(1024)}, f32[768]{0:T(1024)S(1)}, u32[]{:S(2)}) copy-start(f32[768]{0:T(1024)S(1)} %convert_element_type.116) | copy-start | bytes 9220
  104.1 39.3 %copy-start.7 = (bf16[1024,12,32]{0,2,1:T(8,128)(2,1)}, bf16[1024,12,32]{0,2,1:T(8,128)(2,1)S(1)}, u32[]{:S(2)}) copy-start(bf16[1024,12,32]{0,2,1:T(8,128)(2,1)S(1)} %get-tuple-element.108) | copy-start | bytes 2359300
  104.1 39.3 %copy-start.9 = (bf16[1024,12,32]{0,2,1:T(8,128)(2,1)}, bf16[1024,12,32]{0,2,1:T(8,128)(2,1)S(1)}, u32[]{:S(2)}) copy-start(bf16[1024,12,32]{0,2,1:T(8,128)(2,1)S(1)} %get-tuple-element.109) | copy-start | bytes 2359300
  108.2 7.6 copy-start.11
  108.2 7.6 copy-start.12
  109.4 5.2 collective-permute-start
  111.1 4.6 collective-permute-start.2
  132.7 5.6 copy-start
  136.1 7.3 copy-start.42
  146.7 5.6 copy-start.1
  146.7 5.6 copy-start.27
  163.5 60.8 %copy-start.32 = (bf16[1,1024,768]{2,1,0:T(8,128)(2,1)S(1)}, bf16[1,1024,768]{2,1,0:T(8,128)(2,1)}, u32[]{:S(2)}) copy-start(bf16[1,1024,768]{2,1,0:T(8,128)(2,1)} %param.25) | copy-start | bytes 4718596
  224.4 14.9 %copy-start.18 = (f32[1024,2304]{1,0:T(8,128)S(1)}, f32[1024,2304]{1,0:T(8,128)}, u32[]{:S(2)}) copy-start(f32[1024,2304]{1,0:T(8,128)} %fusion.66) | copy-start | bytes 28311556
  243.0 9.3 copy-start.55
  243.0 9.3 copy-start.59
  262.7 23.4 %slice-start = ((s8[15728640]{0:T(1024)(128)(4,1)}), s8[4194304]{0:T(1024)(128)(4,1)S(1)}, s32[]{:S(2)}) async-start(s8[15728640]{0:T(1024)(128)(4,1)} %bitcast.121), calls=%async_computation.12 | async-start | bytes 8388608
  262.7 23.4 %slice-start.1 = ((s8[15728640]{0:T(1024)(128)(4,1)}), s8[4194304]{0:T(1024)(128)(4,1)S(1)}, s32[]{:S(2)}) async-start(s8[15728640]{0:T(1024)(128)(4,1)} %bitcast.121), calls=%async_computation.13 | async-start | bytes 8388608
  262.7 23.4 %slice-start.2 = ((s8[15728640]{0:T(1024)(128)(4,1)}), s8[4194304]{0:T(1024)(128)(4,1)S(1)}, s32[]{:S(2)}) async-start(s8[15728640]{0:T(1024)(128)(4,1)} %bitcast.121), calls=%async_computation.14 | async-start | bytes 8388608
  277.8 8.3 copy-start.43
  277.8 8.4 slice-start.3
  300.0 11.6 %copy-start.8 = (bf16[1024,12,32]{0,2,1:T(8,128)(2,1)S(1)}, bf16[1024,12,32]{0,2,1:T(8,128)(2,1)}, u32[]{:S(2)}) copy-start(bf16[1024,12,32]{0,2,1:T(8,128)(2,1)} %copy-done.7) | copy-start | bytes 2359300
  300.0 11.6 %copy-start.10 = (bf16[1024,12,32]{0,2,1:T(8,128)(2,1)S(1)}, bf16[1024,12,32]{0,2,1:T(8,128)(2,1)}, u32[]{:S(2)}) copy-start(bf16[1024,12,32]{0,2,1:T(8,128)(2,1)} %copy-done.9) | copy-start | bytes 2359300
  326.6 9.8 slice-start.4
  328.7 7.7 slice-start.5
  331.5 8.6 slice-start.6
  331.6 8.5 slice-start.7
  340.1 7.9 copy-start.29
  340.1 7.9 copy-start.33
  345.0 9.9 collective-permute-start.4
  346.8 8.2 collective-permute-start.5
  377.1 6.8 copy-start.54
  786.3 68.1 %reduce-scatter.11.cloned.1.call-start = ((), (), s32[]{:S(2)}) async-start(), calls=%async_computation.11 | async-start | bytes 2211840 | tf_op jit(solution)/shard_map/reduce_scatter | solution.py:229
  786.9 135.4 %reduce-scatter.5.cloned.1.call-start = ((), (), s32[]{:S(2)}) async-start(), calls=%async_computation.8 | async-start | bytes 4423680 | tf_op jit(solution)/shard_map/reduce_scatter | solution.py:220
  787.7 203.8 %reduce-scatter.9.cloned.1.call-start = ((), (), s32[]{:S(2)}) async-start(), calls=%async_computation.10 | async-start | bytes 4423680 | tf_op jit(solution)/shard_map/reduce_scatter | solution.py:226
  (34 other events, 94.0 us)
Sparse Core Ops, SparseCore 0:
  9.6 72.8 all-gather.4
  84.1 29.1 all-gather.6
  114.9 69.0 all-gather.8
  185.4 38.8 all-gather.10
  786.5 27.8 reduce-scatter.6
  817.1 37.2 reduce-scatter.10
  856.9 65.4 reduce-scatter.4
  924.8 66.6 reduce-scatter.8
where the time goes:
time: 1010 us; the launch traced here: 1000 us
  blocking collectives  418 us (41%)
  waiting for transfers between devices  271 us (27%)
  matrix products  141 us (14%)
  other arithmetic  71.9 us (7%)
  local copies, waits for them, and re-layouts  71.7 us (7%)
  between operations  16.7 us (2%)
  starting transfers between devices  10.4 us (1%)
    psum x1, blocking collectives, body(): lax.psum((terms[0], terms[1], terms[2], terms[3], terms[4], terms[5]), 's...  396 us
    reduce_scatter x1, waiting for transfers between devices, body(): lax.psum_scatter(summed[2].astype(jnp.bfloat16), 'wsh', scatter_dimension...  66.6 us
    reduce_scatter x1, waiting for transfers between devices, body(): lax.psum_scatter(summed[0].astype(jnp.bfloat16), 'wsh', scatter_dimension...  65.9 us
    all_gather x1, waiting for transfers between devices, body(): lax.all_gather(w_qkv, 'wsh', axis=0, tiled=True)  48.9 us
    reduce_scatter x1, waiting for transfers between devices, body(): lax.psum_scatter(summed[3].astype(jnp.bfloat16), 'wsh', scatter_dimension...  34.1 us
    all_gather x1, waiting for transfers between devices, body(): lax.all_gather(w_down, 'wsh', axis=0, tiled=True)  29.9 us
    unnamed x145, local copies, waits for them, and re-layouts  26.6 us
    dot_general x2, matrix products, body(): jnp.einsum('qhd,khd->hqk', d_block, value_block, preferred_element_type=j...  24.7 us
  transfers between devices with their start and end apart: 14, of which 7 were waited for; matrix products, arithmetic and copies ran while one was open for 12% of the time, Pallas kernels for 0%

commit v1 on v0

v1 whole, which is shorter than its diff:
```python
import functools

import jax
import jax.numpy as jnp
from jax import lax
from jax.experimental import pallas as pl
from jax.experimental.pallas import tpu as pltpu
from jax.sharding import PartitionSpec as P

HEADS = 12
HALF = 64
HEAD_DIM = 64
PAIR = 2 * HEAD_DIM
EPS = 1e-05
NEGATIVE = -1e30
QROWS = 128
ROWS = 256
SPLIT = 8
VMEM_LIMIT = 56 * 1024 * 1024
F32 = jnp.float32
BF16 = jnp.bfloat16
LAST = (((1,), (1,)), ((), ()))
FIRST = (((0,), (0,)), ((), ()))


def flip(count, bit):
    return [(i, i ^ bit) for i in range(count)]


def orders():
    count = lax.axis_size("seq")
    low = []
    bit = 1
    while bit < min(count, SPLIT):
        low.append(bit)
        bit *= 2
    high = []
    while bit < count:
        high.append(bit)
        bit *= 2
    return low, low[:1] + low[1:][::-1], high


def gather_line(own):
    count = lax.axis_size("wsh")
    here = lax.axis_index("wsh")
    upward = [(i, i + 1) for i in range(count - 1)]
    downward = [(j, i) for i, j in upward]
    ups, downs = [own], [own]
    for _ in range(count - 1):
        ups.append(lax.ppermute(ups[-1], "wsh", upward))
        downs.append(lax.ppermute(downs[-1], "wsh", downward))
    stacked = jnp.stack(ups[:0:-1] + [own] + downs[1:])
    return lax.dynamic_slice_in_dim(stacked, count - 1 - here, count, 0)


def gather_seq(block, order):
    here = lax.axis_index("seq")
    count = lax.axis_size("seq")
    for bit in order[::-1]:
        other = lax.ppermute(block, "seq", flip(count, bit))
        upper = (here & bit) > 0
        block = jnp.concatenate(
            [jnp.where(upper, other, block), jnp.where(upper, block, other)], axis=1
        )
    return block


def own_piece(pieces, order):
    here = lax.axis_index("seq")
    place = jnp.int32(0)
    for bit in order:
        place = place * 2 + jnp.where((here & bit) > 0, 1, 0)
    return lax.dynamic_slice_in_dim(pieces, place, 1, 0)


def gather_weight(pieces):
    first, second, _ = orders()
    half = pieces.shape[2] // 2
    outs = []
    own = [own_piece(pieces[:, :, :half], first), own_piece(pieces[:, :, half:], second)]
    lined = gather_line(jnp.concatenate(own, axis=2))
    outs.append(gather_seq(lined[:, 0][:, None, :, :half], first))
    outs.append(gather_seq(lined[:, 0][:, None, :, half:], second))
    return jnp.concatenate(outs, axis=3)


def reduce_half(block, order, high):
    here = lax.axis_index("seq")
    count = lax.axis_size("seq")
    for bit in order:
        size = block.shape[1] // 2
        upper = (here & bit) > 0
        send = jnp.where(upper, block[:, :size], block[:, size:])
        keep = jnp.where(upper, block[:, size:], block[:, :size])
        block = keep + lax.ppermute(send, "seq", flip(count, bit))
    for bit in high:
        block = block + lax.ppermute(block, "seq", flip(count, bit))
    lines = lax.axis_size("wsh")
    row = lax.axis_index("wsh")
    from_below = from_above = None
    for step in range(lines - 1):
        up = lax.dynamic_slice_in_dim(block, jnp.clip(lines - 1 - step + row, 0, lines - 1), 1, 0)
        down = lax.dynamic_slice_in_dim(block, jnp.clip(step - (lines - 1 - row), 0, lines - 1), 1, 0)
        if step > 0:
            up = up + from_below
            down = down + from_above
        from_below = lax.ppermute(up, "wsh", [(i, i + 1) for i in range(step + 1)])
        from_above = lax.ppermute(
            down, "wsh", [(lines - 1 - i, lines - 2 - i) for i in range(step + 1)]
        )
    own = lax.dynamic_slice_in_dim(block, row, 1, 0)
    total = own + from_below + from_above
    return gather_seq(total, order)[0]


def reduce_grad(block):
    first, second, high = orders()
    half = block.shape[3] // 2
    return jnp.concatenate(
        [
            reduce_half(block[..., :half], first, high),
            reduce_half(block[..., half:], second, high),
        ],
        axis=2,
    )


def fold(block):
    size = block.shape[-2] // 3
    return jnp.concatenate([block[..., i * size : (i + 1) * size, :] for i in range(3)], axis=-1)


def unfold(block):
    width = block.shape[-1] // 3
    return jnp.concatenate([block[..., i * width : (i + 1) * width] for i in range(3)], axis=-2)


def pack(lead, w_in, w_attn, w_down):
    def cut(array):
        return array.reshape(lead + (-1, array.shape[-1]))

    return jnp.concatenate([cut(w_in), fold(cut(w_attn)), fold(cut(w_down))], axis=-2)


def unpack(block, rows_in, rows_attn):
    one = block[..., :rows_in, :]
    two = unfold(block[..., rows_in : rows_in + rows_attn // 3, :])
    three = unfold(block[..., rows_in + rows_attn // 3 :, :])
    return tuple(part.reshape(-1, part.shape[-1]) for part in (one, two, three))


def sum_small(vector):
    for axis in ("seq", "wsh"):
        count = lax.axis_size(axis)
        bit = 1
        while bit < count:
            vector = vector + lax.ppermute(vector, axis, flip(count, bit))
            bit *= 2
    return vector


def neighbours(low_edge, high_edge):
    count = lax.axis_size("seq")
    forward = [(i, i + 1) for i in range(count - 1)]
    backward = [(j, i) for i, j in forward]
    return lax.ppermute(high_edge, "seq", forward), lax.ppermute(low_edge, "seq", backward)


def swap(values):
    lane = lax.broadcasted_iota(jnp.int32, values.shape, 1)
    quarter = HEAD_DIM // 2
    return jnp.where(
        lane % HEAD_DIM < quarter,
        pltpu.roll(values, PAIR - quarter, 1),
        pltpu.roll(values, quarter, 1),
    )


def normalise(values):
    centre = jnp.mean(values, axis=-1, keepdims=True)
    shifted = values - centre
    factor = lax.rsqrt(jnp.mean(shifted * shifted, axis=-1, keepdims=True) + EPS)
    return shifted * factor, factor


def project_kernel(x_ref, gain_ref, w_ref, cos_ref, sin_ref, normed_ref, q_ref, kv_ref):
    width = x_ref.shape[1]
    normed, _ = normalise(x_ref[...].astype(F32))
    low = (normed * gain_ref[...].astype(F32)).astype(BF16)
    normed_ref[...] = low
    cosine, sine = cos_ref[...], sin_ref[...]
    scale = HEAD_DIM ** (-0.5)
    for part in range(2):
        raw = jnp.dot(
            low, w_ref[:, part * width : (part + 1) * width], preferred_element_type=F32
        )
        for start in range(0, width, PAIR):
            piece = raw[:, start : start + PAIR]
            turned = (piece * cosine + swap(piece) * sine).astype(BF16)
            if part == 0:
                q_ref[:, start : start + PAIR] = turned * jnp.asarray(scale, BF16)
            else:
                kv_ref[:, start : start + PAIR] = turned
    kv_ref[:, width:] = jnp.dot(
        low, w_ref[:, 2 * width :], preferred_element_type=F32
    ).astype(BF16)


def both(pair):
    lane = lax.broadcasted_iota(jnp.int32, pair.shape, 1)
    zero = jnp.zeros_like(pair)
    left = jnp.where(lane < HEAD_DIM, pair, zero)
    right = jnp.where(lane < HEAD_DIM, zero, pair)
    return jnp.concatenate([left, right], axis=0)


def merge(stacked):
    rows = stacked.shape[0] // 2
    lane = lax.broadcasted_iota(jnp.int32, (rows, stacked.shape[1]), 1)
    return jnp.where(lane < HEAD_DIM, stacked[:rows], stacked[rows:])


def attend_kernel(q_ref, kv_ref, row_ref, col_ref, context_ref, probs_ref):
    width = q_ref.shape[1]
    span = QROWS + 2 * HALF
    offset = pl.multiple_of(pl.program_id(0) * QROWS, QROWS)
    row = lax.broadcasted_iota(jnp.int32, (QROWS, span), 0)
    col = lax.broadcasted_iota(jnp.int32, (QROWS, span), 1)
    near = (col >= row) & (col <= row + 2 * HALF)
    allowed = near & (row_ref[...] == col_ref[0])
    bias = jnp.where(allowed, 0.0, NEGATIVE)
    bias = jnp.concatenate([bias, bias], axis=0)
    for pair in range(width // PAIR):
        lanes = slice(pair * PAIR, (pair + 1) * PAIR)
        queries = both(q_ref[:, lanes])
        keys = kv_ref[pl.ds(offset, span), lanes]
        values = kv_ref[pl.ds(offset, span), slice(width + pair * PAIR, width + (pair + 1) * PAIR)]
        scores = lax.dot_general(queries, keys, LAST, preferred_element_type=F32)
        scores = jnp.where(bias < 0.0, NEGATIVE, scores)
        raised = jnp.exp(scores - jnp.max(scores, axis=-1, keepdims=True))
        probs = raised * (1.0 / jnp.sum(raised, axis=-1, keepdims=True))
        low = probs.astype(BF16)
        probs_ref[0, pair] = low
        context = jnp.dot(low, values, preferred_element_type=F32)
        context_ref[:, lanes] = merge(context).astype(BF16)


def mlp_kernel(
    x_ref, context_ref, dy_ref, gain_ref, w_attn_ref, w_in_ref, w_down_ref,
    mixed_ref, normed_ref, hidden_ref, d_gate_ref, d_resid_ref, d_low_ref, d_context_ref, d_gain_ref,
):
    hidden_width = w_down_ref.shape[0]
    scales = gain_ref[...].astype(F32)
    resid = x_ref[...].astype(F32) + jnp.dot(
        context_ref[...], w_attn_ref[...], preferred_element_type=F32
    )
    normed, factor = normalise(resid)
    low = (normed * scales).astype(BF16)
    normed_ref[...] = low
    dy = dy_ref[...]
    mixed = resid
    d_normed = jnp.zeros_like(resid)
    step = hidden_width // 3
    for start in range(0, hidden_width, step):
        here = slice(start, start + step)
        there = slice(hidden_width + start, hidden_width + start + step)
        gate = jnp.dot(low, w_in_ref[:, here], preferred_element_type=F32)
        up = jnp.dot(low, w_in_ref[:, there], preferred_element_type=F32)
        d_hidden = lax.dot_general(dy, w_down_ref[here, :], LAST, preferred_element_type=F32)
        cdf = 0.5 + 0.5 * lax.erf(gate * (0.5**0.5))
        pdf = jnp.exp(-0.5 * gate * gate) * 0.3989422804014327
        gelu = gate * cdf
        hidden = (gelu * up).astype(BF16)
        hidden_ref[:, here] = hidden
        mixed = mixed + jnp.dot(hidden, w_down_ref[here, :], preferred_element_type=F32)
        d_gate = (d_hidden * up * (cdf + gate * pdf)).astype(BF16)
        d_up = (d_hidden * gelu).astype(BF16)
        d_gate_ref[:, here] = d_gate
        d_gate_ref[:, there] = d_up
        d_normed = d_normed + lax.dot_general(
            d_gate, w_in_ref[:, here], LAST, preferred_element_type=F32
        )
        d_normed = d_normed + lax.dot_general(
            d_up, w_in_ref[:, there], LAST, preferred_element_type=F32
        )
    mixed_ref[...] = mixed.astype(BF16)
    partial = jnp.sum(d_normed * normed, axis=0, keepdims=True)

    @pl.when(pl.program_id(0) == 0)
    def _():
        d_gain_ref[...] = jnp.zeros_like(d_gain_ref)

    d_gain_ref[...] += partial
    scaled = d_normed * scales
    mean = jnp.mean(scaled, axis=-1, keepdims=True)
    cross = jnp.mean(scaled * normed, axis=-1, keepdims=True)
    d_resid = dy.astype(F32) + factor * (scaled - mean - normed * cross)
    d_resid_ref[...] = d_resid
    d_low = d_resid.astype(BF16)
    d_low_ref[...] = d_low
    d_context_ref[...] = lax.dot_general(
        d_low, w_attn_ref[...], LAST, preferred_element_type=F32
    ).astype(BF16)


def attend_back_kernel(
    q_ref, kv_ref, probs_ref, d_ref, cos_ref, sin_ref, d_q_ref, d_kv_ref
):
    width = q_ref.shape[1]
    span = QROWS + 2 * HALF
    offset = pl.multiple_of(pl.program_id(0) * QROWS, QROWS)

    @pl.when(pl.program_id(0) == 0)
    def _():
        d_kv_ref[...] = jnp.zeros_like(d_kv_ref)

    cosine, sine = cos_ref[...], sin_ref[...]
    scale = HEAD_DIM ** (-0.5)
    for pair in range(width // PAIR):
        lanes = slice(pair * PAIR, (pair + 1) * PAIR)
        value_lanes = slice(width + pair * PAIR, width + (pair + 1) * PAIR)
        queries = both(q_ref[:, lanes])
        d_out = both(d_ref[:, lanes])
        keys = kv_ref[pl.ds(offset, span), lanes]
        values = kv_ref[pl.ds(offset, span), value_lanes]
        low = probs_ref[0, pair]
        probs = low.astype(F32)
        d_probs = lax.dot_general(d_out, values, LAST, preferred_element_type=F32)
        delta = jnp.sum(d_probs * probs, axis=-1, keepdims=True)
        d_scores = (probs * (d_probs - delta)).astype(BF16)
        d_kv_ref[pl.ds(offset, span), value_lanes] += lax.dot_general(
            low, d_out, FIRST, preferred_element_type=F32
        )
        d_kv_ref[pl.ds(offset, span), lanes] += lax.dot_general(
            d_scores, queries, FIRST, preferred_element_type=F32
        )
        d_q = merge(jnp.dot(d_scores, keys, preferred_element_type=F32)) * scale
        d_q_ref[:, lanes] = (d_q * cosine - swap(d_q) * sine).astype(BF16)


def finish_kernel(d_q_ref, d_kv_ref, low_ref, high_ref, cos_ref, sin_ref, d_qkv_ref):
    width = d_q_ref.shape[1]
    step = pl.program_id(0)
    offset = pl.multiple_of(step * ROWS, ROWS)
    first = step == 0
    last = step == pl.num_programs(0) - 1
    cosine, sine = cos_ref[...], sin_ref[...]
    d_qkv_ref[:, :width] = d_q_ref[...]
    for start in range(0, 2 * width, PAIR):
        lanes = slice(start, start + PAIR)
        block = d_kv_ref[pl.ds(offset + HALF, ROWS), lanes]
        low = jnp.where(first, low_ref[:, lanes].astype(F32), 0.0)
        high = jnp.where(last, high_ref[:, lanes].astype(F32), 0.0)
        block = jnp.concatenate(
            [block[:HALF] + low, block[HALF : ROWS - HALF], block[ROWS - HALF :] + high], axis=0
        )
        if start < width:
            block = block * cosine - swap(block) * sine
        d_qkv_ref[:, width + start : width + start + PAIR] = block.astype(BF16)


def norm_back_kernel(x_ref, gain_ref, d_qkv_ref, w_ref, d_resid_ref, d_tokens_ref, d_gain_ref):
    normed, factor = normalise(x_ref[...].astype(F32))
    d_normed = lax.dot_general(d_qkv_ref[...], w_ref[...], LAST, preferred_element_type=F32)
    partial = jnp.sum(d_normed * normed, axis=0, keepdims=True)

    @pl.when(pl.program_id(0) == 0)
    def _():
        d_gain_ref[...] = jnp.zeros_like(d_gain_ref)

    d_gain_ref[...] += partial
    scaled = d_normed * gain_ref[...].astype(F32)
    mean = jnp.mean(scaled, axis=-1, keepdims=True)
    cross = jnp.mean(scaled * normed, axis=-1, keepdims=True)
    d_tokens_ref[...] = d_resid_ref[...] + factor * (scaled - mean - normed * cross)


def by_rows(rows, width):
    return pl.BlockSpec((rows, width), lambda i: (i, 0))


def whole(shape):
    return pl.BlockSpec(shape, lambda i: (0,) * len(shape))


def call(kernel, steps, inputs, specs, outs, out_specs, flops):
    size = sum(a.size * a.dtype.itemsize for a in inputs)
    size += sum(o.size * o.dtype.itemsize for o in outs)
    return pl.pallas_call(
        kernel,
        grid=(steps,),
        in_specs=specs,
        out_specs=out_specs,
        out_shape=outs,
        compiler_params=pltpu.CompilerParams(
            dimension_semantics=("arbitrary",), vmem_limit_bytes=VMEM_LIMIT
        ),
        cost_estimate=pl.CostEstimate(flops=flops, bytes_accessed=size, transcendentals=0),
    )(*inputs)


def shape(dims, dtype):
    return jax.ShapeDtypeStruct(dims, dtype)


def body(tokens, positions, w_qkv, w_attn, w_in, w_down, gain_attn, gain_mlp, grad_out):
    rows, width = tokens.shape[1:]
    lines = lax.axis_size("wsh")
    hidden = w_down.shape[0] * lines
    x = tokens[0]
    dy = grad_out[0]
    places = positions[0]
    seq = lax.axis_index("seq")
    seqs = lax.axis_size("seq")

    split = min(SPLIT, seqs)
    gains = gather_line(jnp.stack([gain_attn, gain_mlp]))
    gain_a = gains[:, 0].reshape(1, width)
    gain_m = gains[:, 1].reshape(1, width)
    full_qkv = gather_weight(w_qkv.reshape(split, -1, 3 * width)).reshape(width, 3 * width)
    packed = gather_weight(pack((split,), w_in, w_attn, w_down))
    rows_in = w_in.shape[0] // split
    rows_attn = w_attn.shape[0] // split
    full_in, full_attn, full_down = unpack(packed, rows_in, rows_attn)

    base = seq * rows
    ids = places - (base + jnp.arange(rows, dtype=jnp.int32))
    below, above = neighbours(ids[:HALF], ids[rows - HALF :])
    nowhere = jnp.int32(-(1 << 30))
    below = jnp.where(seq == 0, nowhere, below)
    above = jnp.where(seq == seqs - 1, nowhere, above)
    ids_wide = jnp.concatenate([below, ids, above])
    blocks = rows // QROWS
    span = QROWS + 2 * HALF
    cols = jnp.stack([ids_wide[i * QROWS : i * QROWS + span] for i in range(blocks)])[:, None, :]

    lane = jnp.arange(PAIR, dtype=jnp.int32)
    quarter = HEAD_DIM // 2
    exponent = (lane % quarter).astype(F32) * (2.0 / HEAD_DIM)
    frequency = jnp.power(F32(10000.0), -exponent)
    angles = places.astype(F32)[:, None] * frequency[None, :]
    cosine = jnp.cos(angles)
    sine = jnp.where(lane % HEAD_DIM < quarter, -1.0, 1.0)[None, :] * jnp.sin(angles)

    big = rows // ROWS
    normed_attn, queries, kv = call(
        project_kernel, big, (x, gain_a, full_qkv, cosine, sine),
        [by_rows(ROWS, width), whole((1, width)), whole((width, 3 * width)),
         by_rows(ROWS, PAIR), by_rows(ROWS, PAIR)],
        [shape((rows, width), BF16), shape((rows, width), BF16), shape((rows, 2 * width), BF16)],
        [by_rows(ROWS, width), by_rows(ROWS, width), by_rows(ROWS, 2 * width)],
        6 * rows * width * width,
    )
    kv_below, kv_above = neighbours(kv[:HALF], kv[rows - HALF :])
    kv_wide = jnp.concatenate([kv_below, kv, kv_above], axis=0)
    pairs = width // PAIR
    probs_spec = pl.BlockSpec((1, pairs, 2 * QROWS, span), lambda i: (i, 0, 0, 0))
    attend_flops = 4 * blocks * pairs * 2 * QROWS * span * PAIR
    context, probs = call(
        attend_kernel, blocks, (queries, kv_wide, ids[:, None], cols),
        [by_rows(QROWS, width), whole((rows + 2 * HALF, 2 * width)), by_rows(QROWS, 1),
         pl.BlockSpec((1, 1, span), lambda i: (i, 0, 0))],
        [shape((rows, width), BF16), shape((blocks, pairs, 2 * QROWS, span), BF16)],
        [by_rows(QROWS, width), probs_spec],
        attend_flops,
    )
    mixed, normed_mlp, hidden_low, d_gate, d_resid, d_low, d_context, d_gain_m = call(
        mlp_kernel, big, (x, context, dy, gain_m, full_attn, full_in, full_down),
        [by_rows(ROWS, width), by_rows(ROWS, width), by_rows(ROWS, width), whole((1, width)),
         whole((width, width)), whole((width, 2 * hidden)), whole((hidden, width))],
        [shape((rows, width), BF16), shape((rows, width), BF16), shape((rows, hidden), BF16),
         shape((rows, 2 * hidden), BF16), shape((rows, width), F32), shape((rows, width), BF16),
         shape((rows, width), BF16), shape((1, width), F32)],
        [by_rows(ROWS, width), by_rows(ROWS, width), by_rows(ROWS, hidden),
         by_rows(ROWS, 2 * hidden), by_rows(ROWS, width), by_rows(ROWS, width),
         by_rows(ROWS, width), whole((1, width))],
        2 * rows * width * (2 * width + 6 * hidden),
    )

    def weight_grad(left, right):
        return lax.dot_general(left, right, FIRST, preferred_element_type=F32).astype(BF16)

    grads_packed = pack(
        (lines, split),
        weight_grad(normed_mlp, d_gate),
        weight_grad(context, d_low),
        weight_grad(hidden_low, dy),
    )
    out_packed = reduce_grad(grads_packed)

    d_q, d_kv = call(
        attend_back_kernel, blocks, (queries, kv_wide, probs, d_context, cosine, sine),
        [by_rows(QROWS, width), whole((rows + 2 * HALF, 2 * width)), probs_spec,
         by_rows(QROWS, width), by_rows(QROWS, PAIR), by_rows(QROWS, PAIR)],
        [shape((rows, width), BF16), shape((rows + 2 * HALF, 2 * width), F32)],
        [by_rows(QROWS, width), whole((rows + 2 * HALF, 2 * width))],
        2 * attend_flops,
    )
    from_below, from_above = neighbours(
        d_kv[:HALF].astype(BF16), d_kv[rows + HALF :].astype(BF16)
    )
    (d_qkv,) = call(
        finish_kernel, big, (d_q, d_kv, from_below, from_above, cosine, sine),
        [by_rows(ROWS, width), whole((rows + 2 * HALF, 2 * width)), whole((HALF, 2 * width)),
         whole((HALF, 2 * width)), by_rows(ROWS, PAIR), by_rows(ROWS, PAIR)],
        [shape((rows, 3 * width), BF16)],
        [by_rows(ROWS, 3 * width)],
        8 * rows * width,
    )
    grad_qkv = weight_grad(normed_attn, d_qkv).reshape(lines, split, -1, 3 * width)
    out_qkv = reduce_grad(grad_qkv).reshape(-1, 3 * width).astype(F32)
    d_tokens, d_gain_a = call(
        norm_back_kernel, big, (x, gain_a, d_qkv, full_qkv, d_resid),
        [by_rows(ROWS, width), whole((1, width)), by_rows(ROWS, 3 * width),
         whole((width, 3 * width)), by_rows(ROWS, width)],
        [shape((rows, width), F32), shape((1, width), F32)],
        [by_rows(ROWS, width), whole((1, width))],
        6 * rows * width * width,
    )
    gain_sums = sum_small(jnp.concatenate([d_gain_a, d_gain_m], axis=0))
    share = width // lines
    gain_own = lax.dynamic_slice_in_dim(
        gain_sums.reshape(2, lines, share), lax.axis_index("wsh"), 1, 1
    )[:, 0]
    out_in, out_attn, out_down = unpack(out_packed, rows_in, rows_attn)
    return (
        mixed[None],
        d_tokens[None],
        out_qkv,
        out_attn.astype(F32),
        out_in.astype(F32),
        out_down.astype(F32),
        gain_own[0],
        gain_own[1],
    )


def solution(mesh):
    rows = P("wsh", "seq", None)
    return jax.shard_map(
        body,
        mesh=mesh,
        in_specs=(
            rows, P("wsh", "seq"), P("wsh", None), P("wsh", None), P("wsh", None),
            P("wsh", None), P("wsh"), P("wsh"), rows,
        ),
        out_specs=(
            rows, rows, P("wsh", None), P("wsh", None), P("wsh", None), P("wsh", None),
            P("wsh"), P("wsh"),
        ),
        check_vma=False,
    )
```

time: 1010 us -> 539 us (0.53)
  blocking collectives: 418 us -> 0 us
  waiting for transfers between devices: 271 us -> 113 us
  starting transfers between devices: 10.4 us -> 157 us
  matrix products: 141 us -> 16.9 us
  Pallas kernels: 0 us -> 97.1 us
  other arithmetic: 71.9 us -> 107 us
  local copies, waits for them, and re-layouts: 71.7 us -> 39.9 us
  between operations: 16.7 us -> 3.26 us
    psum x1 -> x0, blocking collectives: 396 us -> none  [body(): lax.psum((terms[0], terms[1], terms[2], terms[3], terms[4], terms[5]), 's...]
    reduce_scatter x4 -> x0, waiting for transfers between devices: 167 us -> none  [the longest x1 66.6 us: body(): lax.psum_scatter(summed[2].astype(jnp.bfloat16), 'wsh', scatter_dimension...]
    ppermute x6 -> x89, starting transfers between devices: 9.92 us -> 157 us  [the longest x9 41.5 us: gather_line(): ups.append(lax.ppermute(ups[-1], 'wsh', upward))]
    dot_general x24 -> x4, matrix products: 141 us -> 16.9 us  [weight_grad(): lax.dot_general(left, right, FIRST, preferred_element_type=F32).astype(BF16)]
    ppermute x6 -> x89, waiting for transfers between devices: 1.21 us -> 113 us  [the longest x24 37 us: gather_seq(): other = lax.ppermute(block, 'seq', flip(count, bit))]
    all_gather x4 -> x0, waiting for transfers between devices: 99.2 us -> none  [the longest x1 48.9 us: body(): lax.all_gather(w_qkv, 'wsh', axis=0, tiled=True)]
    pallas_call x0 -> x6, Pallas kernels: none -> 97.1 us  [call(): pl.pallas_call(kernel, grid=(steps,), in_specs=specs, out_specs=out_specs...]
    concatenate x5 -> x30, other arithmetic: 5.55 us -> 60.3 us  [the longest x2 27.6 us: pack(): jnp.concatenate([cut(w_in), fold(cut(w_attn)), fold(cut(w_down))], axis=-2)]
  transfers between devices with their start and end apart: 14 -> 89, of which waited for: 7 -> 33; matrix products, arithmetic and copies ran while one was open for 12% -> 20% of each run, Pallas kernels for 0% -> 4%
where the time goes in v1:
time: 539 us; the launch traced here: 534 us
  starting transfers between devices  157 us (29%)
  waiting for transfers between devices  113 us (21%)
  other arithmetic  107 us (20%)
  Pallas kernels  97.1 us (18%)
  local copies, waits for them, and re-layouts  39.9 us (7%)
  matrix products  16.9 us (3%)
    pallas_call x6, Pallas kernels, call(): pl.pallas_call(kernel, grid=(steps,), in_specs=specs, out_specs=out_specs...  97.1 us
    ppermute x9, starting transfers between devices, gather_line(): ups.append(lax.ppermute(ups[-1], 'wsh', upward))  41.5 us
    ppermute x24, waiting for transfers between devices, gather_seq(): other = lax.ppermute(block, 'seq', flip(count, bit))  37 us
    ppermute x12, starting transfers between devices, reduce_half(): from_below = lax.ppermute(up, 'wsh', [(i, i + 1) for i in range(step + 1)])  36.6 us
    ppermute x12, waiting for transfers between devices, reduce_half(): lax.ppermute(down, 'wsh', [(lines - 1 - i, lines - 2 - i) for i in range(...  35.1 us
    concatenate x2, other arithmetic, pack(): jnp.concatenate([cut(w_in), fold(cut(w_attn)), fold(cut(w_down))], axis=-2)  27.6 us
    ppermute x24, starting transfers between devices, gather_seq(): other = lax.ppermute(block, 'seq', flip(count, bit))  23.3 us
    ppermute x12, waiting for transfers between devices, reduce_half(): block = keep + lax.ppermute(send, 'seq', flip(count, bit))  18.1 us
  transfers between devices with their start and end apart: 89, of which 33 were waited for; matrix products, arithmetic and copies ran while one was open for 20% of the time, Pallas kernels for 4%

profile of v1, /device:TPU:0, one launch (start us, length us, event | category | flops | bytes accessed | tf_op | source)
XLA Modules:
  0.0 534.0 jit_solution(8838275823511764574)
XLA Ops:
  3.4 5.6 %collective-permute-start = (bf16[2,192]{1,0:T(2,128)(2,1)S(1)}, bf16[2,192]{1,0:T(2,128)(2,1)S(1)}, u32[]{:S(2)}, u32[]{:S(2)}) collective-permute-start(bf16[2,192]{1,0:T(2,128)(2,1)S(1)} %pad_maximum_fusion.25), channel_id=1, source_target_pairs={{0,1},{1,2},{2,3},{4,5},{5,6},{6,7},{8,9},{9,10},{10,11},{12,13},{... | collective-permute-start | bytes 2312 | tf_op jit(solution)/shard_map/ppermute | solution.py:51
  13.0 4.6 collective-permute-start.22
  20.2 3.1 fusion.23
  23.3 3.0 collective-permute-start.20
  28.4 4.5 collective-permute-start.1
  34.4 4.5 collective-permute-start.2
  39.6 3.9 collective-permute-start.6
  45.8 4.4 collective-permute-start.7
  52.5 4.3 collective-permute-start.8
  58.2 4.6 collective-permute-start.23
  64.2 5.2 collective-permute-done.11
  69.5 4.5 collective-permute-start.12
  77.1 5.1 collective-permute-start.24
  87.9 6.1 %collective-permute-done.13 = bf16[4,2,24,1152]{3,2,0,1:T(8,128)(2,1)S(1)} collective-permute-done((bf16[4,2,24,1152]{3,2,0,1:T(8,128)(2,1)S(1)}, bf16[4,2,24,1152]{3,2,0,1:T(8,128)(2,1)S(1)}, u32[]{:S(2)}, u32[]{:S(2)}) %collective-permute-start.13) | collective-permute-done | bytes 442400 | tf_op jit(solution)/shard_map/ppermute | solution.py:61
  102.4 13.7 %collective-permute-done.32 = bf16[4,2,44,1152]{3,0,2,1:T(4,128)(2,1)S(1)} collective-permute-done((bf16[4,2,44,1152]{3,0,2,1:T(4,128)(2,1)S(1)}, bf16[4,2,44,1152]{3,0,2,1:T(4,128)(2,1)S(1)}, u32[]{:S(2)}, u32[]{:S(2)}) %collective-permute-start.32) | collective-permute-done | bytes 811040 | tf_op jit(solution)/shard_map/ppermute | solution.py:61
  125.7 8.8 %shard_map.152 = (bf16[1024,768]{1,0:T(8,128)(2,1)}, bf16[1024,768]{1,0:T(8,128)(2,1)}, bf16[1024,1536]{1,0:T(8,128)(2,1)}) custom-call(bf16[1024,768]{1,0:T(8,128)(2,1)} %bitcast.161, bf16[1,768]{1,0:T(2,128)(2,1)} %reshape_squeeze.6.gain_ref, bf16[768,2304]{1,0:T(8,128)(2,1)} %bitcast.133, f32[1024,128]{1,0:T(8,128)} %get-tuple-element.137.cos_ref, ...), custom_call_target="tpu_custom_call" | custom-call | flops 3623878656 | bytes 12453376 | tf_op jit(solution)/shard_map/pallas_call | solution.py:390
  146.1 13.9 %shard_map.153 = (bf16[1024,768]{1,0:T(8,128)(2,1)}, bf16[8,6,256,256]{3,2,1,0:T(8,128)(2,1)}) custom-call(bf16[1024,768]{1,0:T(8,128)(2,1)} %get-tuple-element.25.q_ref, bf16[1152,1536]{1,0:T(8,128)(2,1)} %copy-done.5, s32[1024,1]{1,0:T(8,128)} %add_subtract_fusion.row_ref, s32[8,1,256]{2,1,0:T(1,128)} %broadcast_in_dim.43.col_ref), custom_call_target="tpu_custom_call" | custom-call | flops 1610612736 | bytes 12988416 | tf_op jit(solution)/shard_map/pallas_call | solution.py:390
  160.0 3.4 broadcast_select_fusion.7
  163.4 3.4 broadcast_select_fusion.9
  166.8 7.8 %fusion.14 = bf16[4,8,24,768]{3,0,2,1:T(4,128)(2,1)S(1)} fusion(bf16[4,4,44,1152]{3,0,2,1:T(4,128)(2,1)S(1)} %get-tuple-element.57, bf16[4,4,44,1152]{3,0,2,1:T(4,128)(2,1)S(1)} %get-tuple-element.56, bf16[4,4,44,1152]{3,0,2,1:T(4,128)(2,1)S(1)} %get-tuple-element.55, bf16[4,4,44,1152]{3,0,2,1:T(4,128)(2,1)S(1)} %get-tuple-element.54), kind=kLoop, calls=%fused_computation.53 | loop fusion | flops 17104896 | bytes 7667712 | tf_op jit(solution)/shard_map/concatenate | solution.py:136
  175.9 9.5 %maximum_maximum_fusion = bf16[4,8,44,2304]{3,0,2,1:T(4,128)(2,1)S(1)} fusion(bf16[4,4,44,1152]{3,0,2,1:T(4,128)(2,1)S(1)} %get-tuple-element.57, bf16[4,4,44,1152]{3,0,2,1:T(4,128)(2,1)S(1)} %get-tuple-element.56, bf16[4,4,44,1152]{3,0,2,1:T(4,128)(2,1)S(1)} %get-tuple-element.55, bf16[4,4,44,1152]{3,0,2,1:T(4,128)(2,1)S(1)} %get-tuple-element.54), kind=kLoop, calls=%fused_computation | loop fusion | flops 25952256 | bytes 12976128 | tf_op jit(solution)/shard_map/concatenate | solution.py:85
  191.5 26.9 %shard_map.154 = (bf16[1024,768]{1,0:T(8,128)(2,1)}, bf16[1024,768]{1,0:T(8,128)(2,1)}, bf16[1024,1152]{1,0:T(8,128)(2,1)}, bf16[1024,2304]{1,0:T(8,128)(2,1)}, ...) custom-call(bf16[1024,768]{1,0:T(8,128)(2,1)} %bitcast.162, ...), custom_call_target="tpu_custom_call" | custom-call | flops 13287555072 | bytes 27726336 | tf_op jit(solution)/shard_map/pallas_call | solution.py:390
  218.4 2.8 convolution_convert_fusion.3
  224.6 3.3 convolution_convert_fusion.2
  232.1 27.1 %shard_map.155 = (bf16[1024,768]{1,0:T(8,128)(2,1)}, f32[1152,1536]{1,0:T(8,128)}) custom-call(bf16[1024,768]{1,0:T(8,128)(2,1)} %get-tuple-element.25.q_ref, bf16[1152,1536]{1,0:T(8,128)(2,1)} %copy-done.5, bf16[8,6,256,256]{3,2,1,0:T(8,128)(2,1)} %get-tuple-element.29.probs_ref, bf16[1024,768]{1,0:T(8,128)(2,1)} %get-tuple-element.30.d_ref, ...), custom_call_target="tpu_custom_call" | custom-call | flops 3221225472 | bytes 22675456 | tf_op jit(solution)/shard_map/pallas_call | solution.py:390
  259.2 3.6 convert.7
  264.1 7.0 %collective-permute-start.34 = (bf16[64,1536]{1,0:T(8,128)(2,1)S(1)}, bf16[64,1536]{1,0:T(8,128)(2,1)}, u32[]{:S(2)}, u32[]{:S(2)}) collective-permute-start(bf16[64,1536]{1,0:T(8,128)(2,1)S(1)} %get-tuple-element.53), channel_id=1, source_target_pairs={{0,4},{4,8},{8,12},{12,16},{16,20},{20,24},{24,28},{1,5},{5,9},{9,... | collective-permute-start | bytes 589832 | tf_op jit(solution)/shard_map/ppermute | solution.py:167
  271.0 4.1 convolution_convert_fusion
  275.2 2.7 copy.373
  278.0 27.4 %maximum_maximum_fusion.1 = bf16[4,8,44,2304]{3,0,2,1:T(4,128)(2,1)S(1)} fusion(bf16[4,8,12,768]{3,0,2,1:T(4,128)(2,1)S(1)} %copy.398, bf16[4,8,12,768]{3,0,2,1:T(4,128)(2,1)S(1)} %copy.397, bf16[4,8,12,768]{3,0,2,1:T(4,128)(2,1)S(1)} %copy.396, bf16[4,8,8,768]{3,0,2,1:T(4,128)(2,1)S(1)} %copy-done.8, bf16[4,8,8,768]{3,0,2,1:T(4,128)(2,1)S(1)} %copy-done.7, ...), kind=kLoop, calls=%fused_computation.1 | loop fusion | flops 45416448 | bytes 12976128 | tf_op jit(solution)/shard_map/concatenate | solution.py:143
  305.4 10.0 %shard_map.156.d_qkv_ref = bf16[1024,2304]{1,0:T(8,128)(2,1)} custom-call(bf16[1024,768]{1,0:T(8,128)(2,1)} %get-tuple-element.31.d_q_ref, f32[1152,1536]{1,0:T(8,128)} %get-tuple-element.32.d_kv_ref, bf16[64,1536]{1,0:T(8,128)(2,1)} %collective-permute-done.34.low_ref, bf16[64,1536]{1,0:T(8,128)(2,1)} %collective-permute-done.35.high_ref, ...), custom_call_target="tpu_custom_call" | custom-call | flops 6291456 | bytes 14811136 | tf_op jit(solution)/shard_map/pallas_call | solution.py:390
  315.4 10.5 %shard_map.157 = (f32[1024,768]{1,0:T(8,128)}, f32[1,768]{1,0:T(1,128)}) custom-call(bf16[1024,768]{1,0:T(8,128)(2,1)} %bitcast.163, bf16[1,768]{1,0:T(2,128)(2,1)} %reshape_squeeze.6.gain_ref, bf16[1024,2304]{1,0:T(8,128)(2,1)} %shard_map.156.d_qkv_ref, bf16[768,2304]{1,0:T(8,128)(2,1)} %bitcast.134, f32[1024,768]{1,0:T(8,128)} %get-tuple-element.33.d_resid_ref), custom_call_target="tpu_custom_call" | custom-call | flops 3623878656 | bytes 16126464 | tf_op jit(solution)/shard_map/pallas_call | solution.py:390
  327.8 6.6 %convolution_convert_fusion.1 = bf16[768,2304]{1,0:T(8,128)(2,1)S(1)} fusion(bf16[1024,768]{1,0:T(8,128)(2,1)S(1)} %copy-done.16, bf16[1024,2304]{1,0:T(8,128)(2,1)} %shard_map.156.d_qkv_ref), kind=kOutput, calls=%fused_computation.5 | convolution fusion | flops 3625648128 | bytes 9830400 | tf_op jit(solution)/shard_map/dot_general | solution.py:482
  334.4 3.5 collective-permute-start.85
  351.8 3.4 collective-permute-done.88
  361.4 7.3 %collective-permute-done.49 = bf16[4,2,24,1152]{3,2,0,1:T(8,128)(2,1)S(1)} collective-permute-done((bf16[4,2,24,1152]{3,2,0,1:T(8,128)(2,1)S(1)}, bf16[4,2,24,1152]{3,2,0,1:T(8,128)(2,1)S(1)}, u32[]{:S(2)}, u32[]{:S(2)}) %collective-permute-start.49) | collective-permute-done | bytes 442400 | tf_op jit(solution)/shard_map/ppermute | solution.py:96
  374.2 5.3 copy_add_fusion.1
  387.2 4.3 collective-permute-start.52
  393.4 4.3 collective-permute-start.53
  405.4 18.6 %collective-permute-done.56 = bf16[1,1,24,1152]{3,2,0,1:T(8,128)(2,1)S(1)} collective-permute-done((bf16[1,1,24,1152]{3,2,0,1:T(8,128)(2,1)S(1)}, bf16[1,1,24,1152]{3,2,0,1:T(8,128)(2,1)S(1)}, u32[]{:S(2)}, u32[]{:S(2)}) %collective-permute-start.56) | collective-permute-done | bytes 55328 | tf_op jit(solution)/shard_map/ppermute | solution.py:109
  441.6 8.8 %collective-permute-done.74 = bf16[4,1,44,1152]{3,0,2,1:T(4,128)(2,1)S(1)} collective-permute-done((bf16[4,1,44,1152]{3,0,2,1:T(4,128)(2,1)S(1)}, bf16[4,1,44,1152]{3,0,2,1:T(4,128)(2,1)S(1)}, u32[]{:S(2)}, u32[]{:S(2)}) %collective-permute-start.74) | collective-permute-done | bytes 405536 | tf_op jit(solution)/shard_map/ppermute | solution.py:96
  450.9 3.9 collective-permute-start.75
  456.6 3.6 collective-permute-done.75
  460.6 4.4 collective-permute-start.76
  465.3 3.4 collective-permute-start.64
  470.8 4.4 collective-permute-start.77
  476.4 3.2 collective-permute-start.65
  485.7 13.0 %collective-permute-done.80 = bf16[1,1,44,1152]{3,0,2,1:T(2,128)(2,1)S(1)} collective-permute-done((bf16[1,1,44,1152]{3,0,2,1:T(2,128)(2,1)S(1)}, bf16[1,1,44,1152]{3,0,2,1:T(2,128)(2,1)S(1)}, u32[]{:S(2)}, u32[]{:S(2)}) %collective-permute-start.80) | collective-permute-done | bytes 101408 | tf_op jit(solution)/shard_map/ppermute | solution.py:109
  (386 shorter events, 183.5 us)
Async XLA Ops:
  2.1 31.0 %collective-permute-start.3 = (bf16[2,192]{1,0:T(2,128)(2,1)S(1)}, bf16[2,192]{1,0:T(2,128)(2,1)S(1)}, u32[]{:S(2)}, u32[]{:S(2)}) collective-permute-start(bf16[2,192]{1,0:T(2,128)(2,1)S(1)} %pad_maximum_fusion.25), channel_id=1, source_target_pairs={{1,0},{2,1},{3,2},{5,4},{6,5},{7,6},{9,8},{10,9},{11,10},{13,12},{... | collective-permute-start | bytes 2312 | tf_op jit(solution)/shard_map/ppermute | solution.py:52
  3.4 25.1 %collective-permute-start = (bf16[2,192]{1,0:T(2,128)(2,1)S(1)}, bf16[2,192]{1,0:T(2,128)(2,1)S(1)}, u32[]{:S(2)}, u32[]{:S(2)}) collective-permute-start(bf16[2,192]{1,0:T(2,128)(2,1)S(1)} %pad_maximum_fusion.25), channel_id=1, source_target_pairs={{0,1},{1,2},{2,3},{4,5},{5,6},{6,7},{8,9},{9,10},{10,11},{12,13},{... | collective-permute-start | bytes 2312 | tf_op jit(solution)/shard_map/ppermute | solution.py:51
  11.6 45.3 %collective-permute-start.25 = (bf16[1,44,2304]{2,1,0:T(8,128)(2,1)S(1)}, bf16[1,44,2304]{2,1,0:T(8,128)(2,1)S(1)}, u32[]{:S(2)}, u32[]{:S(2)}) collective-permute-start(bf16[1,44,2304]{2,1,0:T(8,128)(2,1)S(1)} %pad_maximum_fusion.18), channel_id=1, source_target_pairs={{1,0},{2,1},{3,2},{5,4},{6,5},{7,6},{9,8},{10,9},{11,10},{13,12},{... | collective-permute-start | bytes 608264 | tf_op jit(solution)/shard_map/ppermute | solution.py:52
  13.0 45.2 %collective-permute-start.22 = (bf16[1,44,2304]{2,1,0:T(8,128)(2,1)S(1)}, bf16[1,44,2304]{2,1,0:T(8,128)(2,1)S(1)}, u32[]{:S(2)}, u32[]{:S(2)}) collective-permute-start(bf16[1,44,2304]{2,1,0:T(8,128)(2,1)S(1)} %pad_maximum_fusion.18), channel_id=1, source_target_pairs={{0,1},{1,2},{2,3},{4,5},{5,6},{6,7},{8,9},{9,10},{10,11},{12,13},{... | collective-permute-start | bytes 608264 | tf_op jit(solution)/shard_map/ppermute | solution.py:51
  27.1 23.1 %collective-permute-start.9 = (bf16[1,24,2304]{2,1,0:T(8,128)(2,1)S(1)}, bf16[1,24,2304]{2,1,0:T(8,128)(2,1)S(1)}, u32[]{:S(2)}, u32[]{:S(2)}) collective-permute-start(bf16[1,24,2304]{2,1,0:T(8,128)(2,1)S(1)} %pad_maximum_fusion.21), channel_id=1, source_target_pairs={{1,0},{2,1},{3,2},{5,4},{6,5},{7,6},{9,8},{10,9},{11,10},{13,12},{... | collective-permute-start | bytes 331784 | tf_op jit(solution)/shard_map/ppermute | solution.py:52
  34.4 9.1 %collective-permute-start.2 = (bf16[2,192]{1,0:T(2,128)(2,1)S(1)}, bf16[2,192]{1,0:T(2,128)(2,1)S(1)}, u32[]{:S(2)}, u32[]{:S(2)}) collective-permute-start(bf16[2,192]{1,0:T(2,128)(2,1)S(1)} %collective-permute-done.1), channel_id=1, source_target_pairs={{0,1},{1,2},{2,3},{4,5},{5,6},{6,7},{8,9},{9,10},{10,11},{12,13},{... | collective-permute-start | bytes 2312 | tf_op jit(solution)/shard_map/ppermute | solution.py:51
  43.5 30.6 %collective-permute-start.5 = (bf16[2,192]{1,0:T(2,128)(2,1)S(1)}, bf16[2,192]{1,0:T(2,128)(2,1)S(1)}, u32[]{:S(2)}, u32[]{:S(2)}) collective-permute-start(bf16[2,192]{1,0:T(2,128)(2,1)S(1)} %collective-permute-done.4), channel_id=1, source_target_pairs={{1,0},{2,1},{3,2},{5,4},{6,5},{7,6},{9,8},{10,9},{11,10},{13,12},{... | collective-permute-start | bytes 2312 | tf_op jit(solution)/shard_map/ppermute | solution.py:52
  50.2 12.5 %collective-permute-start.10 = (bf16[1,24,2304]{2,1,0:T(8,128)(2,1)S(1)}, bf16[1,24,2304]{2,1,0:T(8,128)(2,1)S(1)}, u32[]{:S(2)}, u32[]{:S(2)}) collective-permute-start(bf16[1,24,2304]{2,1,0:T(8,128)(2,1)S(1)} %collective-permute-done.9), channel_id=1, source_target_pairs={{1,0},{2,1},{3,2},{5,4},{6,5},{7,6},{9,8},{10,9},{11,10},{13,12},{... | collective-permute-start | bytes 331784 | tf_op jit(solution)/shard_map/ppermute | solution.py:52
  52.5 11.5 %collective-permute-start.8 = (bf16[1,24,2304]{2,1,0:T(8,128)(2,1)S(1)}, bf16[1,24,2304]{2,1,0:T(8,128)(2,1)S(1)}, u32[]{:S(2)}, u32[]{:S(2)}) collective-permute-start(bf16[1,24,2304]{2,1,0:T(8,128)(2,1)S(1)} %collective-permute-done.7), channel_id=1, source_target_pairs={{0,1},{1,2},{2,3},{4,5},{5,6},{6,7},{8,9},{9,10},{10,11},{12,13},{... | collective-permute-start | bytes 331784 | tf_op jit(solution)/shard_map/ppermute | solution.py:51
  56.9 19.0 %collective-permute-start.26 = (bf16[1,44,2304]{2,1,0:T(8,128)(2,1)S(1)}, bf16[1,44,2304]{2,1,0:T(8,128)(2,1)S(1)}, u32[]{:S(2)}, u32[]{:S(2)}) collective-permute-start(bf16[1,44,2304]{2,1,0:T(8,128)(2,1)S(1)} %collective-permute-done.25), channel_id=1, source_target_pairs={{1,0},{2,1},{3,2},{5,4},{6,5},{7,6},{9,8},{10,9},{11,10},{13,12},{... | collective-permute-start | bytes 608264 | tf_op jit(solution)/shard_map/ppermute | solution.py:52
  58.2 18.9 %collective-permute-start.23 = (bf16[1,44,2304]{2,1,0:T(8,128)(2,1)S(1)}, bf16[1,44,2304]{2,1,0:T(8,128)(2,1)S(1)}, u32[]{:S(2)}, u32[]{:S(2)}) collective-permute-start(bf16[1,44,2304]{2,1,0:T(8,128)(2,1)S(1)} %collective-permute-done.22), channel_id=1, source_target_pairs={{0,1},{1,2},{2,3},{4,5},{5,6},{6,7},{8,9},{9,10},{10,11},{12,13},{... | collective-permute-start | bytes 608264 | tf_op jit(solution)/shard_map/ppermute | solution.py:51
  69.5 12.7 %collective-permute-start.12 = (bf16[4,1,24,1152]{3,2,0,1:T(8,128)(2,1)S(1)}, bf16[4,1,24,1152]{3,2,0,1:T(8,128)(2,1)S(1)}, u32[]{:S(2)}, u32[]{:S(2)}) collective-permute-start(bf16[4,1,24,1152]{3,2,0,1:T(8,128)(2,1)S(1)} %get-tuple-element.109), channel_id=1, source_target_pairs={{0,16},{4,20},{8,24},{12,28},{16,0},{20,4},{24,8},{28,12},{1,17},{... | collective-permute-start | bytes 663560 | tf_op jit(solution)/shard_map/ppermute | solution.py:61
  75.8 9.4 %collective-permute-start.27 = (bf16[1,44,2304]{2,1,0:T(8,128)(2,1)S(1)}, bf16[1,44,2304]{2,1,0:T(8,128)(2,1)S(1)}, u32[]{:S(2)}, u32[]{:S(2)}) collective-permute-start(bf16[1,44,2304]{2,1,0:T(8,128)(2,1)S(1)} %collective-permute-done.26), channel_id=1, source_target_pairs={{1,0},{2,1},{3,2},{5,4},{6,5},{7,6},{9,8},{10,9},{11,10},{13,12},{... | collective-permute-start | bytes 608264 | tf_op jit(solution)/shard_map/ppermute | solution.py:52
  82.3 11.6 %collective-permute-start.13 = (bf16[4,2,24,1152]{3,2,0,1:T(8,128)(2,1)S(1)}, bf16[4,2,24,1152]{3,2,0,1:T(8,128)(2,1)S(1)}, u32[]{:S(2)}, u32[]{:S(2)}) collective-permute-start(bf16[4,2,24,1152]{3,2,0,1:T(8,128)(2,1)S(1)} %pad_maximum_fusion.12), channel_id=1, source_target_pairs={{0,8},{4,12},{8,0},{12,4},{16,24},{20,28},{24,16},{28,20},{1,9},{5... | collective-permute-start | bytes 1327112 | tf_op jit(solution)/shard_map/ppermute | solution.py:61
  84.2 16.7 %collective-permute-start.16 = (bf16[4,2,24,1152]{3,2,1,0:T(8,128)(2,1)S(1)}, bf16[4,2,24,1152]{3,2,1,0:T(8,128)(2,1)S(1)}, u32[]{:S(2)}, u32[]{:S(2)}) collective-permute-start(bf16[4,2,24,1152]{3,2,1,0:T(8,128)(2,1)S(1)} %pad_maximum_fusion.13), channel_id=1, source_target_pairs={{0,16},{4,20},{8,24},{12,28},{16,0},{20,4},{24,8},{28,12},{1,17},{... | collective-permute-start | bytes 1327112 | tf_op jit(solution)/shard_map/ppermute | solution.py:61
  86.1 10.8 %collective-permute-start.28 = (bf16[4,1,44,1152]{3,0,2,1:T(4,128)(2,1)S(1)}, bf16[4,1,44,1152]{3,0,2,1:T(4,128)(2,1)S(1)}, u32[]{:S(2)}, u32[]{:S(2)}) collective-permute-start(bf16[4,1,44,1152]{3,0,2,1:T(4,128)(2,1)S(1)} %get-tuple-element.96), channel_id=1, source_target_pairs={{0,16},{4,20},{8,24},{12,28},{16,0},{20,4},{24,8},{28,12},{1,17},{... | collective-permute-start | bytes 1216520 | tf_op jit(solution)/shard_map/ppermute | solution.py:61
  87.3 11.0 %collective-permute-start.31 = (bf16[4,1,44,1152]{3,0,2,1:T(4,128)(2,1)S(1)}, bf16[4,1,44,1152]{3,0,2,1:T(4,128)(2,1)S(1)}, u32[]{:S(2)}, u32[]{:S(2)}) collective-permute-start(bf16[4,1,44,1152]{3,0,2,1:T(4,128)(2,1)S(1)} %get-tuple-element.97), channel_id=1, source_target_pairs={{0,8},{4,12},{8,0},{12,4},{16,24},{20,28},{24,16},{28,20},{1,9},{5... | collective-permute-start | bytes 1216520 | tf_op jit(solution)/shard_map/ppermute | solution.py:61
  94.2 29.1 %collective-permute-start.14 = (bf16[4,4,24,1152]{3,2,0,1:T(8,128)(2,1)S(1)}, bf16[4,4,24,1152]{3,2,0,1:T(8,128)(2,1)S(1)}, u32[]{:S(2)}, u32[]{:S(2)}) collective-permute-start(bf16[4,4,24,1152]{3,2,0,1:T(8,128)(2,1)S(1)} %pad_maximum_fusion.6), channel_id=1, source_target_pairs={{0,4},{4,0},{8,12},{12,8},{16,20},{20,16},{24,28},{28,24},{1,5},{5... | collective-permute-start | bytes 2654216 | tf_op jit(solution)/shard_map/ppermute | solution.py:61
  99.6 16.5 %collective-permute-start.32 = (bf16[4,2,44,1152]{3,0,2,1:T(4,128)(2,1)S(1)}, bf16[4,2,44,1152]{3,0,2,1:T(4,128)(2,1)S(1)}, u32[]{:S(2)}, u32[]{:S(2)}) collective-permute-start(bf16[4,2,44,1152]{3,0,2,1:T(4,128)(2,1)S(1)} %pad_maximum_fusion.9), channel_id=1, source_target_pairs={{0,16},{4,20},{8,24},{12,28},{16,0},{20,4},{24,8},{28,12},{1,17},{... | collective-permute-start | bytes 2433032 | tf_op jit(solution)/shard_map/ppermute | solution.py:61
  101.1 22.4 %collective-permute-start.17 = (bf16[4,4,24,1152]{3,2,1,0:T(8,128)(2,1)S(1)}, bf16[4,4,24,1152]{3,2,1,0:T(8,128)(2,1)S(1)}, u32[]{:S(2)}, u32[]{:S(2)}) collective-permute-start(bf16[4,4,24,1152]{3,2,1,0:T(8,128)(2,1)S(1)} %pad_maximum_fusion.7), channel_id=1, source_target_pairs={{0,4},{4,0},{8,12},{12,8},{16,20},{20,16},{24,28},{28,24},{1,5},{5... | collective-permute-start | bytes 2654216 | tf_op jit(solution)/shard_map/ppermute | solution.py:61
  101.8 20.5 %collective-permute-start.29 = (bf16[4,2,44,1152]{3,0,2,1:T(4,128)(2,1)S(1)}, bf16[4,2,44,1152]{3,0,2,1:T(4,128)(2,1)S(1)}, u32[]{:S(2)}, u32[]{:S(2)}) collective-permute-start(bf16[4,2,44,1152]{3,0,2,1:T(4,128)(2,1)S(1)} %pad_maximum_fusion.8), channel_id=1, source_target_pairs={{0,8},{4,12},{8,0},{12,4},{16,24},{20,28},{24,16},{28,20},{1,9},{5... | collective-permute-start | bytes 2433032 | tf_op jit(solution)/shard_map/ppermute | solution.py:61
  119.9 40.1 %collective-permute-start.33 = (bf16[4,4,44,1152]{3,1,2,0:T(4,128)(2,1)}, bf16[4,4,44,1152]{3,1,2,0:T(4,128)(2,1)}, u32[]{:S(2)}, u32[]{:S(2)}) collective-permute-start(bf16[4,4,44,1152]{3,1,2,0:T(4,128)(2,1)} %copy.357), channel_id=1, source_target_pairs={{0,4},{4,0},{8,12},{12,8},{16,20},{20,16},{24,28},{28,24},{1,5},{5... | collective-permute-start | bytes 4866056 | tf_op jit(solution)/shard_map/ppermute | solution.py:61
  140.1 23.4 %collective-permute-start.30 = (bf16[4,4,44,1152]{3,1,2,0:T(4,128)(2,1)}, bf16[4,4,44,1152]{3,1,2,0:T(4,128)(2,1)}, u32[]{:S(2)}, u32[]{:S(2)}) collective-permute-start(bf16[4,4,44,1152]{3,1,2,0:T(4,128)(2,1)} %copy.354), channel_id=1, source_target_pairs={{0,4},{4,0},{8,12},{12,8},{16,20},{20,16},{24,28},{28,24},{1,5},{5... | collective-permute-start | bytes 4866056 | tf_op jit(solution)/shard_map/ppermute | solution.py:61
  262.8 42.6 %collective-permute-start.35 = (bf16[64,1536]{1,0:T(8,128)(2,1)S(1)}, bf16[64,1536]{1,0:T(8,128)(2,1)}, u32[]{:S(2)}, u32[]{:S(2)}) collective-permute-start(bf16[64,1536]{1,0:T(8,128)(2,1)S(1)} %get-tuple-element.52), channel_id=1, source_target_pairs={{4,0},{8,4},{12,8},{16,12},{20,16},{24,20},{28,24},{5,1},{9,5},{13... | collective-permute-start | bytes 589832 | tf_op jit(solution)/shard_map/ppermute | solution.py:167
  264.1 41.3 %collective-permute-start.34 = (bf16[64,1536]{1,0:T(8,128)(2,1)S(1)}, bf16[64,1536]{1,0:T(8,128)(2,1)}, u32[]{:S(2)}, u32[]{:S(2)}) collective-permute-start(bf16[64,1536]{1,0:T(8,128)(2,1)S(1)} %get-tuple-element.53), channel_id=1, source_target_pairs={{0,4},{4,8},{8,12},{12,16},{16,20},{20,24},{24,28},{1,5},{5,9},{9,... | collective-permute-start | bytes 589832 | tf_op jit(solution)/shard_map/ppermute | solution.py:167
  341.1 14.8 %collective-permute-start.48 = (bf16[4,4,24,1152]{3,2,0,1:T(8,128)(2,1)}, bf16[4,4,24,1152]{3,2,0,1:T(8,128)(2,1)}, u32[]{:S(2)}, u32[]{:S(2)}) collective-permute-start(bf16[4,4,24,1152]{3,2,0,1:T(8,128)(2,1)} %broadcast_select_fusion.13), channel_id=1, source_target_pairs={{0,4},{4,0},{8,12},{12,8},{16,20},{20,16},{24,28},{28,24},{1,5},{5... | collective-permute-start | bytes 2654216 | tf_op jit(solution)/shard_map/ppermute | solution.py:96
  350.1 24.1 %collective-permute-start.72 = (bf16[4,4,44,1152]{3,1,2,0:T(4,128)(2,1)}, bf16[4,4,44,1152]{3,1,2,0:T(4,128)(2,1)}, u32[]{:S(2)}, u32[]{:S(2)}) collective-permute-start(bf16[4,4,44,1152]{3,1,2,0:T(4,128)(2,1)} %copy.380), channel_id=1, source_target_pairs={{0,4},{4,0},{8,12},{12,8},{16,20},{20,16},{24,28},{28,24},{1,5},{5... | collective-permute-start | bytes 4866056 | tf_op jit(solution)/shard_map/ppermute | solution.py:96
  350.1 24.1 %collective-permute-start.60 = (bf16[4,4,44,1152]{3,1,2,0:T(4,128)(2,1)}, bf16[4,4,44,1152]{3,1,2,0:T(4,128)(2,1)}, u32[]{:S(2)}, u32[]{:S(2)}) collective-permute-start(bf16[4,4,44,1152]{3,1,2,0:T(4,128)(2,1)} %copy.374), channel_id=1, source_target_pairs={{0,4},{4,0},{8,12},{12,8},{16,20},{20,16},{24,28},{28,24},{1,5},{5... | collective-permute-start | bytes 4866056 | tf_op jit(solution)/shard_map/ppermute | solution.py:96
  357.7 11.0 %collective-permute-start.49 = (bf16[4,2,24,1152]{3,2,0,1:T(8,128)(2,1)S(1)}, bf16[4,2,24,1152]{3,2,0,1:T(8,128)(2,1)S(1)}, u32[]{:S(2)}, u32[]{:S(2)}) collective-permute-start(bf16[4,2,24,1152]{3,2,0,1:T(8,128)(2,1)S(1)} %broadcast_select_fusion.28), channel_id=1, source_target_pairs={{0,16},{4,20},{8,24},{12,28},{16,0},{20,4},{24,8},{28,12},{1,17},{... | collective-permute-start | bytes 1327112 | tf_op jit(solution)/shard_map/ppermute | solution.py:96
  359.7 13.2 %collective-permute-start.37 = (bf16[4,2,24,1152]{3,2,0,1:T(8,128)(2,1)S(1)}, bf16[4,2,24,1152]{3,2,0,1:T(8,128)(2,1)S(1)}, u32[]{:S(2)}, u32[]{:S(2)}) collective-permute-start(bf16[4,2,24,1152]{3,2,0,1:T(8,128)(2,1)S(1)} %broadcast_select_fusion.29), channel_id=1, source_target_pairs={{0,8},{4,12},{8,0},{12,4},{16,24},{20,28},{24,16},{28,20},{1,9},{5... | collective-permute-start | bytes 1327112 | tf_op jit(solution)/shard_map/ppermute | solution.py:96
  368.8 14.1 %collective-permute-start.50 = (bf16[4,1,24,1152]{3,2,0,1:T(8,128)(2,1)S(1)}, bf16[4,1,24,1152]{3,2,0,1:T(8,128)(2,1)S(1)}, u32[]{:S(2)}, u32[]{:S(2)}) collective-permute-start(bf16[4,1,24,1152]{3,2,0,1:T(8,128)(2,1)S(1)} %broadcast_select_fusion.46), channel_id=1, source_target_pairs={{0,8},{4,12},{8,0},{12,4},{16,24},{20,28},{24,16},{28,20},{1,9},{5... | collective-permute-start | bytes 663560 | tf_op jit(solution)/shard_map/ppermute | solution.py:96
  373.0 12.3 %collective-permute-start.38 = (bf16[4,1,24,1152]{3,2,0,1:T(8,128)(2,1)S(1)}, bf16[4,1,24,1152]{3,2,0,1:T(8,128)(2,1)S(1)}, u32[]{:S(2)}, u32[]{:S(2)}) collective-permute-start(bf16[4,1,24,1152]{3,2,0,1:T(8,128)(2,1)S(1)} %broadcast_select_fusion.47), channel_id=1, source_target_pairs={{0,16},{4,20},{8,24},{12,28},{16,0},{20,4},{24,8},{28,12},{1,17},{... | collective-permute-start | bytes 663560 | tf_op jit(solution)/shard_map/ppermute | solution.py:96
  380.4 57.7 %collective-permute-start.73 = (bf16[4,2,44,1152]{3,0,2,1:T(4,128)(2,1)S(1)}, bf16[4,2,44,1152]{3,0,2,1:T(4,128)(2,1)S(1)}, u32[]{:S(2)}, u32[]{:S(2)}) collective-permute-start(bf16[4,2,44,1152]{3,0,2,1:T(4,128)(2,1)S(1)} %broadcast_select_fusion.20), channel_id=1, source_target_pairs={{0,16},{4,20},{8,24},{12,28},{16,0},{20,4},{24,8},{28,12},{1,17},{... | collective-permute-start | bytes 2433032 | tf_op jit(solution)/shard_map/ppermute | solution.py:96
  381.4 58.4 %collective-permute-start.61 = (bf16[4,2,44,1152]{3,0,2,1:T(4,128)(2,1)S(1)}, bf16[4,2,44,1152]{3,0,2,1:T(4,128)(2,1)S(1)}, u32[]{:S(2)}, u32[]{:S(2)}) collective-permute-start(bf16[4,2,44,1152]{3,0,2,1:T(4,128)(2,1)S(1)} %broadcast_select_fusion.23), channel_id=1, source_target_pairs={{0,8},{4,12},{8,0},{12,4},{16,24},{20,28},{24,16},{28,20},{1,9},{5... | collective-permute-start | bytes 2433032 | tf_op jit(solution)/shard_map/ppermute | solution.py:96
  393.4 10.4 %collective-permute-start.53 = (bf16[1,1,24,1152]{3,2,0,1:T(8,128)(2,1)S(1)}, bf16[1,1,24,1152]{3,2,0,1:T(8,128)(2,1)S(1)}, u32[]{:S(2)}, u32[]{:S(2)}) collective-permute-start(bf16[1,1,24,1152]{3,2,0,1:T(8,128)(2,1)S(1)} %get-tuple-element.128), channel_id=1, source_target_pairs={{0,1},{1,2},{2,3},{4,5},{5,6},{6,7},{8,9},{9,10},{10,11},{12,13},{... | collective-permute-start | bytes 165896 | tf_op jit(solution)/shard_map/ppermute | solution.py:108
  398.5 26.4 %collective-permute-start.41 = (bf16[1,1,24,1152]{3,2,0,1:T(8,128)(2,1)S(1)}, bf16[1,1,24,1152]{3,2,0,1:T(8,128)(2,1)S(1)}, u32[]{:S(2)}, u32[]{:S(2)}) collective-permute-start(bf16[1,1,24,1152]{3,2,0,1:T(8,128)(2,1)S(1)} %get-tuple-element.124), channel_id=1, source_target_pairs={{0,1},{1,2},{2,3},{4,5},{5,6},{6,7},{8,9},{9,10},{10,11},{12,13},{... | collective-permute-start | bytes 165896 | tf_op jit(solution)/shard_map/ppermute | solution.py:108
  402.5 21.4 %collective-permute-start.56 = (bf16[1,1,24,1152]{3,2,0,1:T(8,128)(2,1)S(1)}, bf16[1,1,24,1152]{3,2,0,1:T(8,128)(2,1)S(1)}, u32[]{:S(2)}, u32[]{:S(2)}) collective-permute-start(bf16[1,1,24,1152]{3,2,0,1:T(8,128)(2,1)S(1)} %dynamic-slice_add_fusion.9), channel_id=1, source_target_pairs={{3,2},{2,1},{1,0},{7,6},{6,5},{5,4},{11,10},{10,9},{9,8},{15,14},{... | collective-permute-start | bytes 165896 | tf_op jit(solution)/shard_map/ppermute | solution.py:109
  403.8 22.0 %collective-permute-start.44 = (bf16[1,1,24,1152]{3,2,0,1:T(8,128)(2,1)S(1)}, bf16[1,1,24,1152]{3,2,0,1:T(8,128)(2,1)S(1)}, u32[]{:S(2)}, u32[]{:S(2)}) collective-permute-start(bf16[1,1,24,1152]{3,2,0,1:T(8,128)(2,1)S(1)} %dynamic-slice_add_fusion.13), channel_id=1, source_target_pairs={{3,2},{2,1},{1,0},{7,6},{6,5},{5,4},{11,10},{10,9},{9,8},{15,14},{... | collective-permute-start | bytes 165896 | tf_op jit(solution)/shard_map/ppermute | solution.py:109
  438.9 11.5 %collective-permute-start.74 = (bf16[4,1,44,1152]{3,0,2,1:T(4,128)(2,1)S(1)}, bf16[4,1,44,1152]{3,0,2,1:T(4,128)(2,1)S(1)}, u32[]{:S(2)}, u32[]{:S(2)}) collective-permute-start(bf16[4,1,44,1152]{3,0,2,1:T(4,128)(2,1)S(1)} %broadcast_select_fusion.36), channel_id=1, source_target_pairs={{0,8},{4,12},{8,0},{12,4},{16,24},{20,28},{24,16},{28,20},{1,9},{5... | collective-permute-start | bytes 1216520 | tf_op jit(solution)/shard_map/ppermute | solution.py:96
  440.5 14.3 %collective-permute-start.62 = (bf16[4,1,44,1152]{3,0,2,1:T(4,128)(2,1)S(1)}, bf16[4,1,44,1152]{3,0,2,1:T(4,128)(2,1)S(1)}, u32[]{:S(2)}, u32[]{:S(2)}) collective-permute-start(bf16[4,1,44,1152]{3,0,2,1:T(4,128)(2,1)S(1)} %broadcast_select_fusion.39), channel_id=1, source_target_pairs={{0,16},{4,20},{8,24},{12,28},{16,0},{20,4},{24,8},{28,12},{1,17},{... | collective-permute-start | bytes 1216520 | tf_op jit(solution)/shard_map/ppermute | solution.py:96
  450.9 9.4 %collective-permute-start.75 = (bf16[1,1,44,1152]{3,0,2,1:T(2,128)(2,1)S(1)}, bf16[1,1,44,1152]{3,0,2,1:T(2,128)(2,1)S(1)}, u32[]{:S(2)}, u32[]{:S(2)}) collective-permute-start(bf16[1,1,44,1152]{3,0,2,1:T(2,128)(2,1)S(1)} %constant_dynamic-slice_fusion.4), channel_id=1, source_target_pairs={{0,1},{4,5},{8,9},{12,13},{16,17},{20,21},{24,25},{28,29}} | collective-permute-start | bytes 304136 | tf_op jit(solution)/shard_map/ppermute | solution.py:108
  455.3 9.6 %collective-permute-start.63 = (bf16[1,1,44,1152]{3,0,2,1:T(2,128)(2,1)S(1)}, bf16[1,1,44,1152]{3,0,2,1:T(2,128)(2,1)S(1)}, u32[]{:S(2)}, u32[]{:S(2)}) collective-permute-start(bf16[1,1,44,1152]{3,0,2,1:T(2,128)(2,1)S(1)} %constant_dynamic-slice_fusion.6), channel_id=1, source_target_pairs={{0,1},{4,5},{8,9},{12,13},{16,17},{20,21},{24,25},{28,29}} | collective-permute-start | bytes 304136 | tf_op jit(solution)/shard_map/ppermute | solution.py:108
  460.6 9.8 %collective-permute-start.76 = (bf16[1,1,44,1152]{3,0,2,1:T(2,128)(2,1)S(1)}, bf16[1,1,44,1152]{3,0,2,1:T(2,128)(2,1)S(1)}, u32[]{:S(2)}, u32[]{:S(2)}) collective-permute-start(bf16[1,1,44,1152]{3,0,2,1:T(2,128)(2,1)S(1)} %dynamic-slice_add_fusion.2), channel_id=1, source_target_pairs={{0,1},{1,2},{4,5},{5,6},{8,9},{9,10},{12,13},{13,14},{16,17},{17,1... | collective-permute-start | bytes 304136 | tf_op jit(solution)/shard_map/ppermute | solution.py:108
  465.3 10.6 %collective-permute-start.64 = (bf16[1,1,44,1152]{3,0,2,1:T(2,128)(2,1)S(1)}, bf16[1,1,44,1152]{3,0,2,1:T(2,128)(2,1)S(1)}, u32[]{:S(2)}, u32[]{:S(2)}) collective-permute-start(bf16[1,1,44,1152]{3,0,2,1:T(2,128)(2,1)S(1)} %dynamic-slice_add_fusion.6), channel_id=1, source_target_pairs={{0,1},{1,2},{4,5},{5,6},{8,9},{9,10},{12,13},{13,14},{16,17},{17,1... | collective-permute-start | bytes 304136 | tf_op jit(solution)/shard_map/ppermute | solution.py:108
  470.8 14.9 %collective-permute-start.77 = (bf16[1,1,44,1152]{3,0,2,1:T(2,128)(2,1)S(1)}, bf16[1,1,44,1152]{3,0,2,1:T(2,128)(2,1)S(1)}, u32[]{:S(2)}, u32[]{:S(2)}) collective-permute-start(bf16[1,1,44,1152]{3,0,2,1:T(2,128)(2,1)S(1)} %get-tuple-element.117), channel_id=1, source_target_pairs={{0,1},{1,2},{2,3},{4,5},{5,6},{6,7},{8,9},{9,10},{10,11},{12,13},{... | collective-permute-start | bytes 304136 | tf_op jit(solution)/shard_map/ppermute | solution.py:108
  476.4 23.7 %collective-permute-start.65 = (bf16[1,1,44,1152]{3,0,2,1:T(2,128)(2,1)S(1)}, bf16[1,1,44,1152]{3,0,2,1:T(2,128)(2,1)S(1)}, u32[]{:S(2)}, u32[]{:S(2)}) collective-permute-start(bf16[1,1,44,1152]{3,0,2,1:T(2,128)(2,1)S(1)} %get-tuple-element.113), channel_id=1, source_target_pairs={{0,1},{1,2},{2,3},{4,5},{5,6},{6,7},{8,9},{9,10},{10,11},{12,13},{... | collective-permute-start | bytes 304136 | tf_op jit(solution)/shard_map/ppermute | solution.py:108
  482.5 16.2 %collective-permute-start.80 = (bf16[1,1,44,1152]{3,0,2,1:T(2,128)(2,1)S(1)}, bf16[1,1,44,1152]{3,0,2,1:T(2,128)(2,1)S(1)}, u32[]{:S(2)}, u32[]{:S(2)}) collective-permute-start(bf16[1,1,44,1152]{3,0,2,1:T(2,128)(2,1)S(1)} %dynamic-slice_add_fusion.1), channel_id=1, source_target_pairs={{3,2},{2,1},{1,0},{7,6},{6,5},{5,4},{11,10},{10,9},{9,8},{15,14},{... | collective-permute-start | bytes 304136 | tf_op jit(solution)/shard_map/ppermute | solution.py:109
  484.2 18.3 %collective-permute-start.68 = (bf16[1,1,44,1152]{3,0,2,1:T(2,128)(2,1)S(1)}, bf16[1,1,44,1152]{3,0,2,1:T(2,128)(2,1)S(1)}, u32[]{:S(2)}, u32[]{:S(2)}) collective-permute-start(bf16[1,1,44,1152]{3,0,2,1:T(2,128)(2,1)S(1)} %dynamic-slice_add_fusion.5), channel_id=1, source_target_pairs={{3,2},{2,1},{1,0},{7,6},{6,5},{5,4},{11,10},{10,9},{9,8},{15,14},{... | collective-permute-start | bytes 304136 | tf_op jit(solution)/shard_map/ppermute | solution.py:109
  (64 other events, 489.2 us)

commit v2 on v1

--- a/solution.py
+++ b/solution.py
@@ -23,141 +23,261 @@
 FIRST = (((0,), (0,)), ((), ()))
 
 
-def flip(count, bit):
-    return [(i, i ^ bit) for i in range(count)]
-
-
-def orders():
-    count = lax.axis_size("seq")
-    low = []
-    bit = 1
-    while bit < min(count, SPLIT):
-        low.append(bit)
+MESH = pl.DeviceIdType.MESH
+
+
+def place():
+    here = lax.axis_index("seq")
+    bits, partners = [], []
+    for bit in (1, 2, 4):
+        value = lax.rem(here // bit, 2)
+        bits.append(value)
+        partners.append({"seq": here + bit * (1 - 2 * value)})
+    return here, bits, partners, lax.axis_index("wsh")
+
+
+def greet(targets):
+    barrier = pltpu.get_barrier_semaphore()
+    for target in targets:
+        pl.semaphore_signal(barrier, inc=1, device_id=target, device_id_type=MESH)
+    pl.semaphore_wait(barrier, len(targets))
+
+
+def remote(source, target, send, recv, device):
+    return pltpu.make_async_remote_copy(
+        src_ref=source, dst_ref=target, send_sem=send, recv_sem=recv,
+        device_id=device, device_id_type=MESH,
+    )
+
+
+def half_lanes(ref, which):
+    size = ref.shape[-1] // 2
+    return pl.ds(pl.multiple_of(which * size, 128), size)
+
+
+def gather_kernel(seqs, lines, arrays, *refs):
+    shards, ids = refs[:arrays], refs[arrays]
+    fulls = refs[arrays + 1 : 2 * arrays + 1]
+    below, above = refs[2 * arrays + 1 : 2 * arrays + 3]
+    sends, recvs, locals_, id_send, id_recv = refs[2 * arrays + 3 :]
+    here, bits, partners, row = place()
+    up = {"seq": lax.rem(here + 1, seqs)}
+    down = {"seq": lax.rem(here + seqs - 1, seqs)}
+    others = [{"wsh": lax.rem(row + k, lines)} for k in range(1, lines)]
+    greet(partners + others + [up, down])
+    moves = [
+        remote(ids, below, id_send.at[0], id_recv.at[0], up),
+        remote(ids, above, id_send.at[1], id_recv.at[1], down),
+    ]
+    for move in moves:
+        move.start()
+    keeps = []
+    stages = [[], [], [], []]
+    for a in range(arrays):
+        first, second = (1, 2) if a % 2 == 0 else (2, 1)
+        p, q = bits[first], bits[second]
+        lanes = half_lanes(shards[a], bits[0])
+        for k in range(1, lines):
+            stages[0].append(
+                remote(
+                    shards[a].at[p, q, :, lanes], fulls[a].at[row, p, q, :, lanes],
+                    sends.at[0, a, k - 1], recvs.at[0, a, k - 1], others[k - 1],
+                )
+            )
+            origin = lax.rem(row + lines - k, lines)
+            parts = (
+                fulls[a].at[origin, p, q, :, lanes],
+                fulls[a].at[origin, p, :, :, lanes],
+                fulls[a].at[origin, :, :, :, lanes],
+            )
+            for stage, part, bit in zip((1, 2, 3), parts, (second, first, 0)):
+                stages[stage].append(
+                    remote(
+                        part, part, sends.at[stage, a, k - 1], recvs.at[stage, a, k - 1],
+                        partners[bit],
+                    )
+                )
+        keeps.append(pltpu.make_async_copy(shards[a], fulls[a].at[row], locals_.at[a]))
+    for move in stages[0]:
+        move.start()
+    for keep in keeps:
+        keep.start()
+    for stage in (1, 2, 3):
+        for before, move in zip(stages[stage - 1], stages[stage]):
+            before.wait_recv()
+            move.start()
+    for move in stages[3]:
+        move.wait_recv()
+    for stage in stages:
+        for move in stage:
+            move.wait_send()
+    for keep in keeps:
+        keep.wait()
+    for move in moves:
+        move.wait()
+
+
+def gather_all(shards, ids, collective_id):
+    seqs, lines = lax.axis_size("seq"), lax.axis_size("wsh")
+    count = len(shards)
+    vmem = pl.BlockSpec(memory_space=pltpu.VMEM)
+    outs = [shape((lines,) + s.shape, s.dtype) for s in shards] + [shape(ids.shape, ids.dtype)] * 2
+    return pl.pallas_call(
+        functools.partial(gather_kernel, seqs, lines, count),
+        out_shape=outs,
+        in_specs=[vmem] * (count + 1),
+        out_specs=[vmem] * len(outs),
+        scratch_shapes=[
+            pltpu.SemaphoreType.DMA((4, count, lines - 1)),
+            pltpu.SemaphoreType.DMA((4, count, lines - 1)),
+            pltpu.SemaphoreType.DMA((count,)),
+            pltpu.SemaphoreType.DMA((2,)),
+            pltpu.SemaphoreType.DMA((2,)),
+        ],
+        compiler_params=pltpu.CompilerParams(
+            collective_id=collective_id, has_side_effects=True, vmem_limit_bytes=VMEM_LIMIT
+        ),
+    )(*shards, ids)
+
+
+def reduce_kernel(lines, arrays, *refs):
+    terms, sums = refs[:arrays], refs[arrays : 2 * arrays]
+    buffers = refs[2 * arrays : 7 * arrays]
+    sends, recvs = refs[7 * arrays :]
+    here, bits, partners, row = place()
+    others = [{"wsh": lax.rem(row + k, lines)} for k in range(1, lines)]
+    greet(partners + others)
+    begun = []
+
+    def begin(move):
+        move.start()
+        begun.append(move)
+        return move
+
+    state = []
+    for a in range(arrays):
+        first, second = (1, 2) if a % 2 == 0 else (2, 1)
+        p, q = bits[first], bits[second]
+        total, one, two, three, cross = buffers[5 * a : 5 * a + 5]
+        mine = half_lanes(terms[a], bits[0])
+        theirs = half_lanes(terms[a], 1 - bits[0])
+        state.append((first, second, p, q, total, one, two, three, cross, mine))
+        begin(
+            remote(
+                terms[a].at[:, :, :, :, theirs], one, sends.at[0, a], recvs.at[0, a], partners[0]
+            )
+        )
+    before = list(begun)
+    after = []
+    for a in range(arrays):
+        first, second, p, q, total, one, two, three, cross, mine = state[a]
+        before[a].wait_recv()
+
+        @pl.loop(0, lines * 4)
+        def _(i):
+            z, u, v = i // 4, lax.rem(i // 2, 2), lax.rem(i, 2)
+            total[z, u, v] = (
+                terms[a][z, u, v, :, mine].astype(F32) + one[z, u, v].astype(F32)
+            ).astype(BF16)
+
+        after.append(
+            begin(
+                remote(
+                    total.at[:, 1 - p], two, sends.at[1, a], recvs.at[1, a], partners[first]
+                )
+            )
+        )
+    before, after = after, []
+    for a in range(arrays):
+        first, second, p, q, total, one, two, three, cross, mine = state[a]
+        before[a].wait_recv()
+
+        @pl.loop(0, lines * 2)
+        def _(i):
+            z, v = i // 2, lax.rem(i, 2)
+            total[z, p, v] = (total[z, p, v].astype(F32) + two[z, v].astype(F32)).astype(BF16)
+
+        after.append(
+            begin(
+                remote(
+                    total.at[:, p, 1 - q], three, sends.at[2, a], recvs.at[2, a], partners[second]
+                )
+            )
+        )
+    before, after = after, []
+    for a in range(arrays):
+        first, second, p, q, total, one, two, three, cross, mine = state[a]
+        before[a].wait_recv()
+
+        @pl.loop(0, lines)
+        def _(z):
+            total[z, p, q] = (total[z, p, q].astype(F32) + three[z].astype(F32)).astype(BF16)
+
+        after.append(
+            [
+                begin(
+                    remote(
+                        total.at[lax.rem(row + k, lines), p, q], cross.at[k - 1],
+                        sends.at[2 + k, a], recvs.at[2 + k, a], others[k - 1],
+                    )
+                )
+                for k in range(1, lines)
+            ]
+        )
+    before, after = after, []
+    for a in range(arrays):
+        first, second, p, q, total, one, two, three, cross, mine = state[a]
+        value = total[row, p, q].astype(F32)
+        for k in range(1, lines):
+            before[a][k - 1].wait_recv()
+            value = value + cross[k - 1].astype(F32)
+        sums[a][p, q, :, mine] = value.astype(BF16)
+        part = sums[a].at[p, q, :, mine]
+        after.append(
+            begin(
+                remote(part, part, sends.at[lines + 2, a], recvs.at[lines + 2, a], partners[second])
+            )
+        )
+    for stage, bit in ((lines + 3, 0), (lines + 4, 1)):
+        before, after = after, []
+        for a in range(arrays):
+            first, second, p, q, total, one, two, three, cross, mine = state[a]
+            before[a].wait_recv()
+            part = sums[a].at[p, :, :, mine] if bit == 0 else sums[a].at[:, :, :, mine]
+            target = partners[first] if bit == 0 else partners[0]
+            after.append(begin(remote(part, part, sends.at[stage, a], recvs.at[stage, a], target)))
+    for move in after:
+        move.wait_recv()
+    for move in begun:
+        move.wait_send()
+
+
+def reduce_all(terms, collective_id):
+    lines, seqs = lax.axis_size("wsh"), lax.axis_size("seq")
+    count = len(terms)
+    vmem = pl.BlockSpec(memory_space=pltpu.VMEM)
+    scratch = []
+    for term in terms:
+        r, c = term.shape[3], term.shape[4] // 2
+        for lead in ((lines, 2, 2), (lines, 2, 2), (lines, 2), (lines,), (lines - 1,)):
+            scratch.append(pltpu.VMEM(lead + (r, c), BF16))
+    scratch += [pltpu.SemaphoreType.DMA((lines + 5, count))] * 2
+    sums = pl.pallas_call(
+        functools.partial(reduce_kernel, lines, count),
+        out_shape=[shape(t.shape[1:], BF16) for t in terms],
+        in_specs=[vmem] * count,
+        out_specs=[vmem] * count,
+        scratch_shapes=scratch,
+        compiler_params=pltpu.CompilerParams(
+            collective_id=collective_id, has_side_effects=True, vmem_limit_bytes=VMEM_LIMIT
+        ),
+    )(*terms)
+    bit = SPLIT
+    while bit < seqs:
+        swaps = [(i, i ^ bit) for i in range(seqs)]
+        sums = [s + lax.ppermute(s, "seq", swaps) for s in sums]
         bit *= 2
-    high = []
-    while bit < count:
-        high.append(bit)
-        bit *= 2
-    return low, low[:1] + low[1:][::-1], high
-
-
-def gather_line(own):
-    count = lax.axis_size("wsh")
-    here = lax.axis_index("wsh")
-    upward = [(i, i + 1) for i in range(count - 1)]
-    downward = [(j, i) for i, j in upward]
-    ups, downs = [own], [own]
-    for _ in range(count - 1):
-        ups.append(lax.ppermute(ups[-1], "wsh", upward))
-        downs.append(lax.ppermute(downs[-1], "wsh", downward))
-    stacked = jnp.stack(ups[:0:-1] + [own] + downs[1:])
-    return lax.dynamic_slice_in_dim(stacked, count - 1 - here, count, 0)
-
-
-def gather_seq(block, order):
-    here = lax.axis_index("seq")
-    count = lax.axis_size("seq")
-    for bit in order[::-1]:
-        other = lax.ppermute(block, "seq", flip(count, bit))
-        upper = (here & bit) > 0
-        block = jnp.concatenate(
-            [jnp.where(upper, other, block), jnp.where(upper, block, other)], axis=1
-        )
-    return block
-
-
-def own_piece(pieces, order):
-    here = lax.axis_index("seq")
-    place = jnp.int32(0)
-    for bit in order:
-        place = place * 2 + jnp.where((here & bit) > 0, 1, 0)
-    return lax.dynamic_slice_in_dim(pieces, place, 1, 0)
-
-
-def gather_weight(pieces):
-    first, second, _ = orders()
-    half = pieces.shape[2] // 2
-    outs = []
-    own = [own_piece(pieces[:, :, :half], first), own_piece(pieces[:, :, half:], second)]
-    lined = gather_line(jnp.concatenate(own, axis=2))
-    outs.append(gather_seq(lined[:, 0][:, None, :, :half], first))
-    outs.append(gather_seq(lined[:, 0][:, None, :, half:], second))
-    return jnp.concatenate(outs, axis=3)
-
-
-def reduce_half(block, order, high):
-    here = lax.axis_index("seq")
-    count = lax.axis_size("seq")
-    for bit in order:
-        size = block.shape[1] // 2
-        upper = (here & bit) > 0
-        send = jnp.where(upper, block[:, :size], block[:, size:])
-        keep = jnp.where(upper, block[:, size:], block[:, :size])
-        block = keep + lax.ppermute(send, "seq", flip(count, bit))
-    for bit in high:
-        block = block + lax.ppermute(block, "seq", flip(count, bit))
-    lines = lax.axis_size("wsh")
-    row = lax.axis_index("wsh")
-    from_below = from_above = None
-    for step in range(lines - 1):
-        up = lax.dynamic_slice_in_dim(block, jnp.clip(lines - 1 - step + row, 0, lines - 1), 1, 0)
-        down = lax.dynamic_slice_in_dim(block, jnp.clip(step - (lines - 1 - row), 0, lines - 1), 1, 0)
-        if step > 0:
-            up = up + from_below
-            down = down + from_above
-        from_below = lax.ppermute(up, "wsh", [(i, i + 1) for i in range(step + 1)])
-        from_above = lax.ppermute(
-            down, "wsh", [(lines - 1 - i, lines - 2 - i) for i in range(step + 1)]
-        )
-    own = lax.dynamic_slice_in_dim(block, row, 1, 0)
-    total = own + from_below + from_above
-    return gather_seq(total, order)[0]
-
-
-def reduce_grad(block):
-    first, second, high = orders()
-    half = block.shape[3] // 2
-    return jnp.concatenate(
-        [
-            reduce_half(block[..., :half], first, high),
-            reduce_half(block[..., half:], second, high),
-        ],
-        axis=2,
-    )
-
-
-def fold(block):
-    size = block.shape[-2] // 3
-    return jnp.concatenate([block[..., i * size : (i + 1) * size, :] for i in range(3)], axis=-1)
-
-
-def unfold(block):
-    width = block.shape[-1] // 3
-    return jnp.concatenate([block[..., i * width : (i + 1) * width] for i in range(3)], axis=-2)
-
-
-def pack(lead, w_in, w_attn, w_down):
-    def cut(array):
-        return array.reshape(lead + (-1, array.shape[-1]))
-
-    return jnp.concatenate([cut(w_in), fold(cut(w_attn)), fold(cut(w_down))], axis=-2)
-
-
-def unpack(block, rows_in, rows_attn):
-    one = block[..., :rows_in, :]
-    two = unfold(block[..., rows_in : rows_in + rows_attn // 3, :])
-    three = unfold(block[..., rows_in + rows_attn // 3 :, :])
-    return tuple(part.reshape(-1, part.shape[-1]) for part in (one, two, three))
-
-
-def sum_small(vector):
-    for axis in ("seq", "wsh"):
-        count = lax.axis_size(axis)
-        bit = 1
-        while bit < count:
-            vector = vector + lax.ppermute(vector, axis, flip(count, bit))
-            bit *= 2
-    return vector
+    return sums
 
 
 def neighbours(low_edge, high_edge):
@@ -414,19 +534,37 @@
     seq = lax.axis_index("seq")
     seqs = lax.axis_size("seq")
 
-    split = min(SPLIT, seqs)
-    gains = gather_line(jnp.stack([gain_attn, gain_mlp]))
-    gain_a = gains[:, 0].reshape(1, width)
-    gain_m = gains[:, 1].reshape(1, width)
-    full_qkv = gather_weight(w_qkv.reshape(split, -1, 3 * width)).reshape(width, 3 * width)
-    packed = gather_weight(pack((split,), w_in, w_attn, w_down))
-    rows_in = w_in.shape[0] // split
-    rows_attn = w_attn.shape[0] // split
-    full_in, full_attn, full_down = unpack(packed, rows_in, rows_attn)
+    share = width // lines
+    quarter_rows = w_down.shape[0] // 4
+
+    def quarters(array, lead=()):
+        return array.reshape(lead + (2, 2, -1, array.shape[-1]))
+
+    def with_gains(down, attn_scale, mlp_scale, lead):
+        extra = jnp.stack([attn_scale.reshape(lead + (4, -1)), mlp_scale.reshape(lead + (4, -1))], axis=-2)
+        pads = [(0, 0)] * (len(lead) + 1) + [(0, 6), (0, width - extra.shape[-1])]
+        joined = jnp.concatenate(
+            [down.astype(F32).reshape(lead + (4, quarter_rows, width)), jnp.pad(extra.astype(F32), pads)],
+            axis=-2,
+        )
+        return quarters(joined.reshape(lead + (-1, width)).astype(BF16), lead)
 
     base = seq * rows
     ids = places - (base + jnp.arange(rows, dtype=jnp.int32))
-    below, above = neighbours(ids[:HALF], ids[rows - HALF :])
+    full_qkv, full_in, full_attn, full_down, ids_below, ids_above = gather_all(
+        (quarters(w_qkv), quarters(w_in), quarters(w_attn),
+         with_gains(w_down, gain_attn, gain_mlp, ())),
+        ids.reshape(-1, 128), 0,
+    )
+    full_qkv = full_qkv.reshape(width, 3 * width)
+    full_in = full_in.reshape(width, 2 * hidden)
+    full_attn = full_attn.reshape(width, width)
+    blocks_down = full_down.reshape(lines, 4, -1, width)
+    full_down = blocks_down[:, :, :quarter_rows].reshape(hidden, width)
+    gain_a = blocks_down[:, :, quarter_rows, : share // 4].reshape(1, width)
+    gain_m = blocks_down[:, :, quarter_rows + 1, : share // 4].reshape(1, width)
+    below = ids_below.reshape(-1)[rows - HALF :]
+    above = ids_above.reshape(-1)[:HALF]
     nowhere = jnp.int32(-(1 << 30))
     below = jnp.where(seq == 0, nowhere, below)
     above = jnp.where(seq == seqs - 1, nowhere, above)
@@ -481,13 +619,9 @@
     def weight_grad(left, right):
         return lax.dot_general(left, right, FIRST, preferred_element_type=F32).astype(BF16)
 
-    grads_packed = pack(
-        (lines, split),
-        weight_grad(normed_mlp, d_gate),
-        weight_grad(context, d_low),
-        weight_grad(hidden_low, dy),
-    )
-    out_packed = reduce_grad(grads_packed)
+    grad_in = weight_grad(normed_mlp, d_gate)
+    grad_attn = weight_grad(context, d_low)
+    grad_down = lax.dot_general(hidden_low, dy, FIRST, preferred_element_type=F32)
 
     d_q, d_kv = call(
         attend_back_kernel, blocks, (queries, kv_wide, probs, d_context, cosine, sine),
@@ -508,8 +642,7 @@
         [by_rows(ROWS, 3 * width)],
         8 * rows * width,
     )
-    grad_qkv = weight_grad(normed_attn, d_qkv).reshape(lines, split, -1, 3 * width)
-    out_qkv = reduce_grad(grad_qkv).reshape(-1, 3 * width).astype(F32)
+    grad_qkv = weight_grad(normed_attn, d_qkv)
     d_tokens, d_gain_a = call(
         norm_back_kernel, big, (x, gain_a, d_qkv, full_qkv, d_resid),
         [by_rows(ROWS, width), whole((1, width)), by_rows(ROWS, 3 * width),
@@ -518,21 +651,22 @@
         [by_rows(ROWS, width), whole((1, width))],
         6 * rows * width * width,
     )
-    gain_sums = sum_small(jnp.concatenate([d_gain_a, d_gain_m], axis=0))
-    share = width // lines
-    gain_own = lax.dynamic_slice_in_dim(
-        gain_sums.reshape(2, lines, share), lax.axis_index("wsh"), 1, 1
-    )[:, 0]
-    out_in, out_attn, out_down = unpack(out_packed, rows_in, rows_attn)
+    lead = (lines,)
+    out_qkv, out_in, out_attn, out_down = reduce_all(
+        (quarters(grad_qkv, lead), quarters(grad_in, lead), quarters(grad_attn, lead),
+         with_gains(grad_down, d_gain_a[0], d_gain_m[0], lead)),
+        1,
+    )
+    out_down = out_down.reshape(4, -1, width)
     return (
         mixed[None],
         d_tokens[None],
-        out_qkv,
-        out_attn.astype(F32),
-        out_in.astype(F32),
-        out_down.astype(F32),
-        gain_own[0],
-        gain_own[1],
+        out_qkv.reshape(share, 3 * width).astype(F32),
+        out_attn.reshape(share, width).astype(F32),
+        out_in.reshape(share, 2 * hidden).astype(F32),
+        out_down[:, :quarter_rows].reshape(-1, width).astype(F32),
+        out_down[:, quarter_rows, : share // 4].reshape(-1).astype(F32),
+        out_down[:, quarter_rows + 1, : share // 4].reshape(-1).astype(F32),
     )
 
 

time: 539 us -> 328 us (0.61)
  Pallas kernels: 97.1 us -> 257 us
  starting transfers between devices: 157 us -> 10.3 us
  waiting for transfers between devices: 113 us -> 0.01 us
  other arithmetic: 107 us -> 21.4 us
  local copies, waits for them, and re-layouts: 39.9 us -> 17.4 us
    pallas_call x0 -> x2, Pallas kernels: none -> 163 us  [the longest x1 97.7 us: reduce_all(): pl.pallas_call(functools.partial(reduce_kernel, lines, count), out_shape=...]
    ppermute x83 -> x0, starting transfers between devices: 141 us -> none  [the longest x9 41.5 us: gather_line(): ups.append(lax.ppermute(ups[-1], 'wsh', upward))]
    ppermute x83 -> x0, waiting for transfers between devices: 111 us -> none  [the longest x24 37 us: gather_seq(): other = lax.ppermute(block, 'seq', flip(count, bit))]
    concatenate x29 -> x2, other arithmetic: 60.2 us -> 3.26 us  [with_gains(): jnp.concatenate([down.astype(F32).reshape(lead + (4, quarter_rows, width)...]
    select_n x35 -> x0, other arithmetic: 23.1 us -> none  [the longest x23 17.8 us: gather_seq(): jnp.where(upper, other, block)]
    add x36 -> x0, other arithmetic: 14.2 us -> none  [the longest x11 10.4 us: reduce_half(): block = keep + lax.ppermute(send, 'seq', flip(count, bit))]
    reshape x5 -> x0, local copies, waits for them, and re-layouts: 7.71 us -> none  [the longest x3 6.24 us: cut(): return array.reshape(lead + (-1, array.shape[-1]))]
    concatenate x8 -> x0, local copies, waits for them, and re-layouts: 5.57 us -> none  [the longest x6 4.18 us: gather_seq(): jnp.concatenate([jnp.where(upper, other, block), jnp.where(upper, block,...]
  transfers between devices with their start and end apart: 89 -> 4, of which waited for: 33 -> 0; matrix products, arithmetic and copies ran while one was open for 20% -> 6% of each run, Pallas kernels for 4% -> 0%
where the time goes in v2:
time: 328 us; the launch traced here: 327 us
  Pallas kernels  257 us (78%)
  other arithmetic  21.4 us (7%)
  matrix products  20.4 us (6%)
  local copies, waits for them, and re-layouts  17.4 us (5%)
  starting transfers between devices  10.3 us (3%)
    pallas_call x1, Pallas kernels, reduce_all(): pl.pallas_call(functools.partial(reduce_kernel, lines, count), out_shape=...  97.7 us
    pallas_call x6, Pallas kernels, call(): pl.pallas_call(kernel, grid=(steps,), in_specs=specs, out_specs=out_specs...  93.9 us
    pallas_call x1, Pallas kernels, gather_all(): pl.pallas_call(functools.partial(gather_kernel, seqs, lines, count), out_...  64.9 us
    dot_general x3, matrix products, weight_grad(): lax.dot_general(left, right, FIRST, preferred_element_type=F32).astype(BF16)  15.7 us
    ppermute x2, starting transfers between devices, neighbours(): lax.ppermute(high_edge, 'seq', forward)  7.75 us
  transfers between devices with their start and end apart: 4, of which 0 were waited for; matrix products, arithmetic and copies ran while one was open for 6% of the time, Pallas kernels for 0%

profile of v2, /device:TPU:0, one launch (start us, length us, event | category | flops | bytes accessed | tf_op | source)
XLA Modules:
  0.0 327.0 jit_solution(11571088910848851124)
XLA Ops:
  0.7 0.7 stack_reshape.6
  1.4 0.7 stack_reshape.7
  2.2 0.7 convert_element_type.74
  2.8 1.3 add_subtract_fusion.2.refs_4_
  4.1 1.8 pad_maximum_fusion.1.refs_3_
  6.0 64.9 %shard_map.152 = (bf16[4,2,2,48,2304]{4,3,2,1,0:T(8,128)(2,1)}, bf16[4,2,2,48,2304]{4,3,2,1,0:T(8,128)(2,1)}, bf16[4,2,2,48,768]{4,3,2,1,0:T(8,128)(2,1)}, bf16[...) custom-call(bf16[2,2,48,2304]{3,2,1,0:T(8,128)(2,1)} %bitcast.68, ...), custom_call_target="tpu_custom_call" | custom-call | tf_op jit(solution)/shard_map/pallas_call | solution.py:125
  70.9 0.9 slice_reduce_fusion
  71.8 0.7 reshape_squeeze.8.gain_ref
  72.5 3.0 fusion.1
  75.5 8.9 %shard_map.153 = (bf16[1024,768]{1,0:T(8,128)(2,1)}, bf16[1024,768]{1,0:T(8,128)(2,1)}, bf16[1024,1536]{1,0:T(8,128)(2,1)}) custom-call(bf16[1024,768]{1,0:T(8,128)(2,1)} %bitcast.93, bf16[1,768]{1,0:T(2,128)(2,1)} %reshape_squeeze.8.gain_ref, bf16[768,2304]{1,0:T(8,128)(2,1)} %bitcast.89, f32[1024,128]{1,0:T(8,128)} %get-tuple-element.71.cos_ref, ...), custom_call_target="tpu_custom_call" | custom-call | flops 3623878656 | bytes 12453376 | tf_op jit(solution)/shard_map/pallas_call | solution.py:510
  84.5 1.8 fusion.15
  86.3 1.3 collective-permute-start.1
  87.6 3.2 collective-permute-start
  90.9 1.3 slice.86
  92.2 1.0 copy.31
  93.2 0.8 broadcast_select_fusion
  94.0 0.7 pad_add_fusion
  94.7 0.7 stack.43
  95.4 0.6 broadcast_in_dim.29.col_ref
  96.0 0.7 reshape_squeeze.9.gain_ref
  96.7 1.9 add_subtract_fusion.row_ref
  98.6 0.2 constant_dynamic-update-slice_fusion.1
  98.9 1.8 copy-done.2
  100.6 14.0 %shard_map.154 = (bf16[1024,768]{1,0:T(8,128)(2,1)}, bf16[8,6,256,256]{3,2,1,0:T(8,128)(2,1)}) custom-call(bf16[1024,768]{1,0:T(8,128)(2,1)} %get-tuple-element.37.q_ref, bf16[1152,1536]{1,0:T(8,128)(2,1)} %copy-done.2, s32[1024,1]{1,0:T(8,128)} %add_subtract_fusion.row_ref, s32[8,1,256]{2,1,0:T(1,128)} %broadcast_in_dim.29.col_ref), custom_call_target="tpu_custom_call" | custom-call | flops 1610612736 | bytes 12988416 | tf_op jit(solution)/shard_map/pallas_call | solution.py:510
  114.6 26.5 %shard_map.155 = (bf16[1024,768]{1,0:T(8,128)(2,1)}, bf16[1024,768]{1,0:T(8,128)(2,1)}, bf16[1024,1152]{1,0:T(8,128)(2,1)}, bf16[1024,2304]{1,0:T(8,128)(2,1)}, ...) custom-call(bf16[1024,768]{1,0:T(8,128)(2,1)} %bitcast.94, ...), custom_call_target="tpu_custom_call" | custom-call | flops 13287555072 | bytes 27726336 | tf_op jit(solution)/shard_map/pallas_call | solution.py:510
  141.2 0.7 convert_reduce_fusion
  141.9 2.8 copy.33
  144.8 4.7 %convolution_convert_fusion.2 = bf16[4,4,72,768]{3,2,1,0:T(8,128)(2,1)} fusion(bf16[4,4,72,1024]{3,2,1,0:T(8,128)(2,1)S(1)} %bitcast.63, bf16[1,1024,768]{2,1,0:T(8,128)(2,1)} %param.17), kind=kOutput, calls=%fused_computation.3 | convolution fusion | flops 1812824064 | bytes 5701632 | tf_op jit(solution)/shard_map/dot_general | solution.py:624
  149.4 26.2 %shard_map.156 = (bf16[1024,768]{1,0:T(8,128)(2,1)}, f32[1152,1536]{1,0:T(8,128)}) custom-call(bf16[1024,768]{1,0:T(8,128)(2,1)} %get-tuple-element.37.q_ref, bf16[1152,1536]{1,0:T(8,128)(2,1)} %copy-done.2, bf16[8,6,256,256]{3,2,1,0:T(8,128)(2,1)} %get-tuple-element.45.probs_ref, bf16[1024,768]{1,0:T(8,128)(2,1)} %get-tuple-element.46.d_ref, ...), custom_call_target="tpu_custom_call" | custom-call | flops 3221225472 | bytes 22675456 | tf_op jit(solution)/shard_map/pallas_call | solution.py:510
  175.7 3.6 %convert.29 = bf16[1152,1536]{1,0:T(8,128)(2,1)S(1)} convert(f32[1152,1536]{1,0:T(8,128)} %get-tuple-element.48.d_kv_ref) | non-fusion elementwise | flops 1769472 | bytes 10616832 | tf_op jit(solution)/shard_map/convert.20
  179.3 1.3 collective-permute-start.3
  180.6 4.5 %collective-permute-start.2 = (bf16[64,1536]{1,0:T(8,128)(2,1)S(1)}, bf16[64,1536]{1,0:T(8,128)(2,1)S(1)}, u32[]{:S(2)}, u32[]{:S(2)}) collective-permute-start(bf16[64,1536]{1,0:T(8,128)(2,1)S(1)} %get-tuple-element.67), channel_id=1, source_target_pairs={{0,4},{4,8},{8,12},{12,16},{16,20},{20,24},{24,28},{1,5},{5,9},{9,... | collective-permute-start | bytes 589832 | tf_op jit(solution)/shard_map/ppermute | solution.py:287
  185.2 7.9 %convolution_convert_fusion = bf16[768,2304]{1,0:T(8,128)(2,1)} fusion(bf16[1024,768]{1,0:T(8,128)(2,1)S(1)} %copy-done.15, bf16[1024,2304]{1,0:T(8,128)(2,1)} %get-tuple-element.53), kind=kOutput, calls=%fused_computation | convolution fusion | flops 3625648128 | bytes 9830400 | tf_op jit(solution)/shard_map/dot_general | solution.py:620
  193.0 2.5 convolution_convert_fusion.3
  195.5 0.7 copy-done.8
  196.3 7.7 %shard_map.157.d_qkv_ref = bf16[1024,2304]{1,0:T(8,128)(2,1)} custom-call(bf16[1024,768]{1,0:T(8,128)(2,1)} %get-tuple-element.47.d_q_ref, f32[1152,1536]{1,0:T(8,128)} %get-tuple-element.48.d_kv_ref, bf16[64,1536]{1,0:T(8,128)(2,1)} %copy-done.9, bf16[64,1536]{1,0:T(8,128)(2,1)} %copy-done.8, f32[1024,128]{1,0:T(8,128)} %get-tuple-element.71.cos_ref, ...), custom_call_target="tpu_custom_call" | custom-call | flops 6291456 | bytes 14811136 | tf_op jit(solution)/shard_map/pallas_call | solution.py:510
  204.0 10.5 %shard_map.158 = (f32[1024,768]{1,0:T(8,128)}, f32[1,768]{1,0:T(1,128)}) custom-call(bf16[1024,768]{1,0:T(8,128)(2,1)} %bitcast.95, bf16[1,768]{1,0:T(2,128)(2,1)} %reshape_squeeze.8.gain_ref, bf16[1024,2304]{1,0:T(8,128)(2,1)} %shard_map.157.d_qkv_ref, bf16[768,2304]{1,0:T(8,128)(2,1)} %bitcast.90, f32[1024,768]{1,0:T(8,128)} %get-tuple-element.49.d_resid_ref), custom_call_target="tpu_custom_call" | custom-call | flops 3623878656 | bytes 16126464 | tf_op jit(solution)/shard_map/pallas_call | solution.py:510
  214.5 5.3 %convolution_convert_fusion.1 = bf16[768,2304]{1,0:T(8,128)(2,1)} fusion(bf16[1024,768]{1,0:T(8,128)(2,1)S(1)} %copy-done.14, bf16[1024,2304]{1,0:T(8,128)(2,1)S(1)} %copy-done), kind=kOutput, calls=%fused_computation.1 | convolution fusion | flops 3625648128 | bytes 9830400 | tf_op jit(solution)/shard_map/dot_general | solution.py:620
  220.0 1.4 pad_maximum_fusion
  221.5 97.7 %shard_map.159 = (bf16[2,2,48,2304]{3,2,1,0:T(8,128)(2,1)}, bf16[2,2,48,2304]{3,2,1,0:T(8,128)(2,1)}, bf16[2,2,48,768]{3,2,1,0:T(8,128)(2,1)}, bf16[2,2,80,768]{3,2,1,0:T(8,128)(2,1)}) custom-call(bf16[4,2,2,48,2304]{4,3,2,1,0:T(8,128)(2,1)} %bitcast.61, bf16[4,2,2,48,2304]{4,3,2,1,0:T(8,128)(2,1)} %bitcast.60, bf16[4,2,2,48,768]{4,3,2,1,0:T(8,128)(2,1)} %bitcast.67, ...), custom_call_target="tpu_custom_call" | custom-call | tf_op jit(solution)/shard_map/pallas_call | solution.py:265
  319.2 0.8 fusion.8
  320.0 1.0 slice.89
  321.1 0.6 reshape.157
  321.7 0.6 reshape.156
  322.3 1.0 bitcast_convert_fusion.2
  323.3 0.9 bitcast_convert_fusion.3
  324.2 1.4 bitcast_convert_fusion.1
  325.6 1.4 bitcast_convert_fusion
  (46 shorter events, 0.5 us)
Async XLA Ops:
  75.5 15.3 %copy-start.10 = (s32[1,1024]{1,0:T(1,128)S(1)}, s32[1,1024]{1,0:T(1,128)}, u32[]{:S(2)}) copy-start(s32[1,1024]{1,0:T(1,128)} %param.10) | copy-start | bytes 12292
  75.5 15.3 %copy-start.4 = (bf16[4,2,2,80,768]{4,3,2,1,0:T(8,128)(2,1)S(1)}, bf16[4,2,2,80,768]{4,3,2,1,0:T(8,128)(2,1)}, u32[]{:S(2)}) copy-start(bf16[4,2,2,80,768]{4,3,2,1,0:T(8,128)(2,1)} %get-tuple-element.35) | copy-start | bytes 5898244
  86.3 12.5 %collective-permute-start.1 = (bf16[64,1536]{1,0:T(8,128)(2,1)}, bf16[64,1536]{1,0:T(8,128)(2,1)S(1)}, u32[]{:S(2)}, u32[]{:S(2)}) collective-permute-start(bf16[64,1536]{1,0:T(8,128)(2,1)} %get-tuple-element.68), channel_id=1, source_target_pairs={{4,0},{8,4},{12,8},{16,12},{20,16},{24,20},{28,24},{5,1},{9,5},{13... | collective-permute-start | bytes 589832 | tf_op jit(solution)/shard_map/ppermute | solution.py:287
  87.6 11.0 %collective-permute-start = (bf16[64,1536]{1,0:T(8,128)(2,1)}, bf16[64,1536]{1,0:T(8,128)(2,1)S(1)}, u32[]{:S(2)}, u32[]{:S(2)}) collective-permute-start(bf16[64,1536]{1,0:T(8,128)(2,1)} %get-tuple-element.69), channel_id=1, source_target_pairs={{0,4},{4,8},{8,12},{12,16},{16,20},{20,24},{24,28},{1,5},{5,9},{9,... | collective-permute-start | bytes 589832 | tf_op jit(solution)/shard_map/ppermute | solution.py:287
  90.9 7.7 %copy-start.1 = (bf16[1024,1536]{1,0:T(8,128)(2,1)S(1)}, bf16[1024,1536]{1,0:T(8,128)(2,1)}, u32[]{:S(2)}) copy-start(bf16[1024,1536]{1,0:T(8,128)(2,1)} %get-tuple-element.38) | copy-start | bytes 9437188
  98.8 1.8 copy-start.2
  175.7 9.4 %copy-start.15 = (bf16[1024,768]{1,0:T(8,128)(2,1)S(1)}, bf16[1024,768]{1,0:T(8,128)(2,1)}, u32[]{:S(2)}) copy-start(bf16[1024,768]{1,0:T(8,128)(2,1)} %get-tuple-element.52) | copy-start | bytes 4718596
  179.3 16.2 %collective-permute-start.3 = (bf16[64,1536]{1,0:T(8,128)(2,1)S(1)}, bf16[64,1536]{1,0:T(8,128)(2,1)S(1)}, u32[]{:S(2)}, u32[]{:S(2)}) collective-permute-start(bf16[64,1536]{1,0:T(8,128)(2,1)S(1)} %get-tuple-element.66), channel_id=1, source_target_pairs={{4,0},{8,4},{12,8},{16,12},{20,16},{24,20},{28,24},{5,1},{9,5},{13... | collective-permute-start | bytes 589832 | tf_op jit(solution)/shard_map/ppermute | solution.py:287
  180.6 14.9 %collective-permute-start.2 = (bf16[64,1536]{1,0:T(8,128)(2,1)S(1)}, bf16[64,1536]{1,0:T(8,128)(2,1)S(1)}, u32[]{:S(2)}, u32[]{:S(2)}) collective-permute-start(bf16[64,1536]{1,0:T(8,128)(2,1)S(1)} %get-tuple-element.67), channel_id=1, source_target_pairs={{0,4},{4,8},{8,12},{12,16},{16,20},{20,24},{24,28},{1,5},{5,9},{9,... | collective-permute-start | bytes 589832 | tf_op jit(solution)/shard_map/ppermute | solution.py:287
  185.1 7.9 %copy-start.12 = (bf16[1024,768]{1,0:T(8,128)(2,1)S(1)}, bf16[1024,768]{1,0:T(8,128)(2,1)}, u32[]{:S(2)}) copy-start(bf16[1024,768]{1,0:T(8,128)(2,1)} %get-tuple-element.41.context_ref) | copy-start | bytes 4718596
  185.1 7.9 %copy-start.13 = (bf16[1024,768]{1,0:T(8,128)(2,1)S(1)}, bf16[1024,768]{1,0:T(8,128)(2,1)}, u32[]{:S(2)}) copy-start(bf16[1024,768]{1,0:T(8,128)(2,1)} %get-tuple-element.54) | copy-start | bytes 4718596
  195.5 0.7 copy-start.8
  195.5 0.7 copy-start.9
  204.0 10.5 %copy-start = (bf16[1024,2304]{1,0:T(8,128)(2,1)S(1)}, bf16[1024,2304]{1,0:T(8,128)(2,1)}, u32[]{:S(2)}) copy-start(bf16[1024,2304]{1,0:T(8,128)(2,1)} %shard_map.157.d_qkv_ref) | copy-start | bytes 14155780
  204.0 10.5 %copy-start.14 = (bf16[1024,768]{1,0:T(8,128)(2,1)S(1)}, bf16[1024,768]{1,0:T(8,128)(2,1)}, u32[]{:S(2)}) copy-start(bf16[1024,768]{1,0:T(8,128)(2,1)} %get-tuple-element.51) | copy-start | bytes 4718596
  214.5 5.4 %copy-start.11 = (f32[1,768]{1,0:T(1,128)S(1)}, f32[1,768]{1,0:T(1,128)}, u32[]{:S(2)}) copy-start(f32[1,768]{1,0:T(1,128)} %get-tuple-element.56) | copy-start | bytes 9220
  214.5 5.5 %copy-start.3 = (bf16[4,4,72,768]{3,2,1,0:T(8,128)(2,1)S(1)}, bf16[4,4,72,768]{3,2,1,0:T(8,128)(2,1)}, u32[]{:S(2)}) copy-start(bf16[4,4,72,768]{3,2,1,0:T(8,128)(2,1)} %convolution_convert_fusion.2) | copy-start | bytes 5308420
  319.2 4.2 %copy-start.7 = (bf16[2,2,48,768]{3,2,1,0:T(8,128)(2,1)S(1)}, bf16[2,2,48,768]{3,2,1,0:T(8,128)(2,1)}, u32[]{:S(2)}) copy-start(bf16[2,2,48,768]{3,2,1,0:T(8,128)(2,1)} %get-tuple-element.59) | copy-start | bytes 884740
  319.2 5.1 %copy-start.6 = (bf16[2,2,48,2304]{3,2,1,0:T(8,128)(2,1)S(1)}, bf16[2,2,48,2304]{3,2,1,0:T(8,128)(2,1)}, u32[]{:S(2)}) copy-start(bf16[2,2,48,2304]{3,2,1,0:T(8,128)(2,1)} %get-tuple-element.58) | copy-start | bytes 2654212
  322.3 3.3 copy-start.5

commit v3 on v2

--- a/solution.py
+++ b/solution.py
@@ -140,10 +140,13 @@
     )(*shards, ids)
 
 
-def reduce_kernel(lines, arrays, *refs):
-    terms, sums = refs[:arrays], refs[arrays : 2 * arrays]
-    buffers = refs[2 * arrays : 7 * arrays]
-    sends, recvs = refs[7 * arrays :]
+def reduce_kernel(lines, arrays, extra_in, extra_out, work, *refs):
+    terms, ins = refs[:arrays], refs[arrays : arrays + extra_in]
+    refs = refs[arrays + extra_in :]
+    sums, outs = refs[:arrays], refs[arrays : arrays + extra_out]
+    refs = refs[arrays + extra_out :]
+    buffers = refs[: 5 * arrays]
+    sends, recvs = refs[5 * arrays :]
     here, bits, partners, row = place()
     others = [{"wsh": lax.rem(row + k, lines)} for k in range(1, lines)]
     greet(partners + others)
@@ -169,6 +172,8 @@
         )
     before = list(begun)
     after = []
+    if work is not None:
+        work(0, *ins, *outs)
     for a in range(arrays):
         first, second, p, q, total, one, two, three, cross, mine = state[a]
         before[a].wait_recv()
@@ -187,6 +192,8 @@
                 )
             )
         )
+    if work is not None:
+        work(1, *ins, *outs)
     before, after = after, []
     for a in range(arrays):
         first, second, p, q, total, one, two, three, cross, mine = state[a]
@@ -252,7 +259,7 @@
         move.wait_send()
 
 
-def reduce_all(terms, collective_id):
+def reduce_all(terms, collective_id, work=None, work_in=(), work_out=()):
     lines, seqs = lax.axis_size("wsh"), lax.axis_size("seq")
     count = len(terms)
     vmem = pl.BlockSpec(memory_space=pltpu.VMEM)
@@ -263,21 +270,22 @@
             scratch.append(pltpu.VMEM(lead + (r, c), BF16))
     scratch += [pltpu.SemaphoreType.DMA((lines + 5, count))] * 2
     sums = pl.pallas_call(
-        functools.partial(reduce_kernel, lines, count),
-        out_shape=[shape(t.shape[1:], BF16) for t in terms],
-        in_specs=[vmem] * count,
-        out_specs=[vmem] * count,
+        functools.partial(reduce_kernel, lines, count, len(work_in), len(work_out), work),
+        out_shape=[shape(t.shape[1:], BF16) for t in terms] + list(work_out),
+        in_specs=[vmem] * (count + len(work_in)),
+        out_specs=[vmem] * (count + len(work_out)),
         scratch_shapes=scratch,
         compiler_params=pltpu.CompilerParams(
             collective_id=collective_id, has_side_effects=True, vmem_limit_bytes=VMEM_LIMIT
         ),
-    )(*terms)
+    )(*terms, *work_in)
+    sums, made = sums[:count], sums[count:]
     bit = SPLIT
     while bit < seqs:
         swaps = [(i, i ^ bit) for i in range(seqs)]
         sums = [s + lax.ppermute(s, "seq", swaps) for s in sums]
         bit *= 2
-    return sums
+    return list(sums), made
 
 
 def neighbours(low_edge, high_edge):
@@ -424,27 +432,36 @@
     ).astype(BF16)
 
 
-def attend_back_kernel(
-    q_ref, kv_ref, probs_ref, d_ref, cos_ref, sin_ref, d_q_ref, d_kv_ref
+def attend_back(part, q_ref, kv_ref, probs_ref, d_ref, cos_ref, sin_ref, d_q_ref, d_kv_ref):
+    blocks = probs_ref.shape[0]
+    cut = 3 * blocks // 8
+    if part == 0:
+        d_kv_ref[...] = jnp.zeros_like(d_kv_ref)
+
+    @pl.loop(*((0, cut) if part == 0 else (cut, blocks)))
+    def _(step):
+        attend_back_block(
+            step, q_ref, kv_ref, probs_ref, d_ref, cos_ref, sin_ref, d_q_ref, d_kv_ref
+        )
+
+
+def attend_back_block(
+    step, q_ref, kv_ref, probs_ref, d_ref, cos_ref, sin_ref, d_q_ref, d_kv_ref
 ):
     width = q_ref.shape[1]
     span = QROWS + 2 * HALF
-    offset = pl.multiple_of(pl.program_id(0) * QROWS, QROWS)
-
-    @pl.when(pl.program_id(0) == 0)
-    def _():
-        d_kv_ref[...] = jnp.zeros_like(d_kv_ref)
-
-    cosine, sine = cos_ref[...], sin_ref[...]
+    offset = pl.multiple_of(step * QROWS, QROWS)
+    rows = pl.ds(offset, QROWS)
+    cosine, sine = cos_ref[rows, :], sin_ref[rows, :]
     scale = HEAD_DIM ** (-0.5)
     for pair in range(width // PAIR):
         lanes = slice(pair * PAIR, (pair + 1) * PAIR)
         value_lanes = slice(width + pair * PAIR, width + (pair + 1) * PAIR)
-        queries = both(q_ref[:, lanes])
-        d_out = both(d_ref[:, lanes])
+        queries = both(q_ref[rows, lanes])
+        d_out = both(d_ref[rows, lanes])
         keys = kv_ref[pl.ds(offset, span), lanes]
         values = kv_ref[pl.ds(offset, span), value_lanes]
-        low = probs_ref[0, pair]
+        low = probs_ref[step, pair]
         probs = low.astype(F32)
         d_probs = lax.dot_general(d_out, values, LAST, preferred_element_type=F32)
         delta = jnp.sum(d_probs * probs, axis=-1, keepdims=True)
@@ -456,7 +473,7 @@
             d_scores, queries, FIRST, preferred_element_type=F32
         )
         d_q = merge(jnp.dot(d_scores, keys, preferred_element_type=F32)) * scale
-        d_q_ref[:, lanes] = (d_q * cosine - swap(d_q) * sine).astype(BF16)
+        d_q_ref[rows, lanes] = (d_q * cosine - swap(d_q) * sine).astype(BF16)
 
 
 def finish_kernel(d_q_ref, d_kv_ref, low_ref, high_ref, cos_ref, sin_ref, d_qkv_ref):
@@ -540,11 +557,11 @@
     def quarters(array, lead=()):
         return array.reshape(lead + (2, 2, -1, array.shape[-1]))
 
-    def with_gains(down, attn_scale, mlp_scale, lead):
+    def with_gains(down, attn_scale, mlp_scale, lead, more=8):
         extra = jnp.stack([attn_scale.reshape(lead + (4, -1)), mlp_scale.reshape(lead + (4, -1))], axis=-2)
-        pads = [(0, 0)] * (len(lead) + 1) + [(0, 6), (0, width - extra.shape[-1])]
+        pads = [(0, 0)] * (len(lead) + 1) + [(0, more - 2), (0, width - extra.shape[-1])]
         joined = jnp.concatenate(
-            [down.astype(F32).reshape(lead + (4, quarter_rows, width)), jnp.pad(extra.astype(F32), pads)],
+            [down.astype(F32).reshape(lead + (4, -1, width)), jnp.pad(extra.astype(F32), pads)],
             axis=-2,
         )
         return quarters(joined.reshape(lead + (-1, width)).astype(BF16), lead)
@@ -623,13 +640,12 @@
     grad_attn = weight_grad(context, d_low)
     grad_down = lax.dot_general(hidden_low, dy, FIRST, preferred_element_type=F32)
 
-    d_q, d_kv = call(
-        attend_back_kernel, blocks, (queries, kv_wide, probs, d_context, cosine, sine),
-        [by_rows(QROWS, width), whole((rows + 2 * HALF, 2 * width)), probs_spec,
-         by_rows(QROWS, width), by_rows(QROWS, PAIR), by_rows(QROWS, PAIR)],
-        [shape((rows, width), BF16), shape((rows + 2 * HALF, 2 * width), F32)],
-        [by_rows(QROWS, width), whole((rows + 2 * HALF, 2 * width))],
-        2 * attend_flops,
+    lead = (lines,)
+    (out_in, out_down, out_attn), (d_q, d_kv) = reduce_all(
+        (quarters(grad_in, lead), with_gains(grad_down, d_gain_m[0], d_gain_m[0], lead),
+         quarters(grad_attn, lead)),
+        1, attend_back, (queries, kv_wide, probs, d_context, cosine, sine),
+        (shape((rows, width), BF16), shape((rows + 2 * HALF, 2 * width), F32)),
     )
     from_below, from_above = neighbours(
         d_kv[:HALF].astype(BF16), d_kv[rows + HALF :].astype(BF16)
@@ -651,21 +667,25 @@
         [by_rows(ROWS, width), whole((1, width))],
         6 * rows * width * width,
     )
-    lead = (lines,)
-    out_qkv, out_in, out_attn, out_down = reduce_all(
-        (quarters(grad_qkv, lead), quarters(grad_in, lead), quarters(grad_attn, lead),
-         with_gains(grad_down, d_gain_a[0], d_gain_m[0], lead)),
-        1,
+    (out_qk, out_v), _ = reduce_all(
+        (quarters(grad_qkv[:, : 2 * width], lead),
+         with_gains(grad_qkv[:, 2 * width :], d_gain_a[0], d_gain_a[0], lead, 16)),
+        2,
+    )
+    out_v = out_v.reshape(4, -1, width)
+    rows_v = share // 4
+    out_qkv = jnp.concatenate(
+        [out_qk.reshape(share, 2 * width), out_v[:, :rows_v].reshape(share, width)], axis=1
     )
     out_down = out_down.reshape(4, -1, width)
     return (
         mixed[None],
         d_tokens[None],
-        out_qkv.reshape(share, 3 * width).astype(F32),
+        out_qkv.astype(F32),
         out_attn.reshape(share, width).astype(F32),
         out_in.reshape(share, 2 * hidden).astype(F32),
         out_down[:, :quarter_rows].reshape(-1, width).astype(F32),
-        out_down[:, quarter_rows, : share // 4].reshape(-1).astype(F32),
+        out_v[:, rows_v, : share // 4].reshape(-1).astype(F32),
         out_down[:, quarter_rows + 1, : share // 4].reshape(-1).astype(F32),
     )
 

time: 328 us -> 351 us (1.070)
  Pallas kernels: 257 us -> 273 us
  local copies, waits for them, and re-layouts: 17.4 us -> 21.1 us
    pallas_call x1 -> x2, Pallas kernels: 97.7 us -> 140 us  [reduce_all(): pl.pallas_call(functools.partial(reduce_kernel, lines, count, len(work_in...]
    pallas_call x6 -> x5, Pallas kernels: 93.9 us -> 67.8 us  [call(): pl.pallas_call(kernel, grid=(steps,), in_specs=specs, out_specs=out_specs...]
  transfers between devices with their start and end apart: 4 -> 4, of which waited for: 0 -> 1; matrix products, arithmetic and copies ran while one was open for 6% -> 3% of each run, Pallas kernels for 0% -> 0%
where the time goes in v3:
time: 351 us; the launch traced here: 350 us
  Pallas kernels  273 us (78%)
  other arithmetic  24.4 us (7%)
  matrix products  22.2 us (6%)
  local copies, waits for them, and re-layouts  21.1 us (6%)
  starting transfers between devices  8.66 us (2%)
    pallas_call x2, Pallas kernels, reduce_all(): pl.pallas_call(functools.partial(reduce_kernel, lines, count, len(work_in...  140 us
    pallas_call x5, Pallas kernels, call(): pl.pallas_call(kernel, grid=(steps,), in_specs=specs, out_specs=out_specs...  67.8 us
    pallas_call x1, Pallas kernels, gather_all(): pl.pallas_call(functools.partial(gather_kernel, seqs, lines, count), out_...  64.8 us
    dot_general x3, matrix products, weight_grad(): lax.dot_general(left, right, FIRST, preferred_element_type=F32).astype(BF16)  18.1 us
  transfers between devices with their start and end apart: 4, of which 1 were waited for; matrix products, arithmetic and copies ran while one was open for 3% of the time, Pallas kernels for 0%

profile of v3, /device:TPU:0, one launch (start us, length us, event | category | flops | bytes accessed | tf_op | source)
XLA Modules:
  0.0 350.1 jit_solution(10839077668730649279)
XLA Ops:
  0.7 0.7 stack_reshape.6
  1.4 0.7 stack_reshape.7
  2.2 0.7 convert_element_type.76
  2.8 1.3 add_subtract_fusion.2.refs_4_
  4.1 1.8 pad_maximum_fusion.2.refs_3_
  6.0 64.8 %shard_map.152 = (bf16[4,2,2,48,2304]{4,3,2,1,0:T(8,128)(2,1)}, bf16[4,2,2,48,2304]{4,3,2,1,0:T(8,128)(2,1)}, bf16[4,2,2,48,768]{4,3,2,1,0:T(8,128)(2,1)}, bf16[...) custom-call(bf16[2,2,48,2304]{3,2,1,0:T(8,128)(2,1)} %bitcast.73, ...), custom_call_target="tpu_custom_call" | custom-call | tf_op jit(solution)/shard_map/pallas_call | solution.py:125
  70.8 0.9 slice_reduce_fusion
  72.4 3.1 fusion.6
  75.4 8.9 %shard_map.153 = (bf16[1024,768]{1,0:T(8,128)(2,1)}, bf16[1024,768]{1,0:T(8,128)(2,1)}, bf16[1024,1536]{1,0:T(8,128)(2,1)}) custom-call(bf16[1024,768]{1,0:T(8,128)(2,1)} %bitcast.101, bf16[1,768]{1,0:T(2,128)(2,1)} %reshape_squeeze.8.gain_ref, bf16[768,2304]{1,0:T(8,128)(2,1)} %bitcast.97, f32[1024,128]{1,0:T(8,128)} %get-tuple-element.71.cos_ref.refs_7_, ...), custom_call_target="tpu_custom_call" | custom-call | flops 3623878656 | bytes 12453376 | tf_op jit(solution)/shard_map/pallas_call | solution.py:527
  84.4 1.8 fusion.21
  86.2 1.3 collective-permute-start.1
  87.4 3.0 collective-permute-start
  90.5 1.3 slice.98
  91.9 1.0 copy.35
  92.9 0.8 broadcast_select_fusion
  93.6 0.7 pad_add_fusion
  94.3 0.7 stack.47
  95.7 0.7 reshape_squeeze.9.gain_ref
  96.4 1.9 add_subtract_fusion.row_ref
  98.5 1.8 copy-done.2
  100.3 13.9 %shard_map.154 = (bf16[1024,768]{1,0:T(8,128)(2,1)}, bf16[8,6,256,256]{3,2,1,0:T(8,128)(2,1)}) custom-call(bf16[1024,768]{1,0:T(8,128)(2,1)} %get-tuple-element.38.q_ref.refs_3_, bf16[1152,1536]{1,0:T(8,128)(2,1)} %copy-done.2, s32[1024,1]{1,0:T(8,128)} %add_subtract_fusion.row_ref, s32[8,1,256]{2,1,0:T(1,128)} %broadcast_in_dim.29.col_ref), custom_call_target="tpu_custom_call" | custom-call | flops 1610612736 | bytes 12988416 | tf_op jit(solution)/shard_map/pallas_call | solution.py:527
  114.2 26.7 %shard_map.155 = (bf16[1024,768]{1,0:T(8,128)(2,1)}, bf16[1024,768]{1,0:T(8,128)(2,1)}, bf16[1024,1152]{1,0:T(8,128)(2,1)}, bf16[1024,2304]{1,0:T(8,128)(2,1)}, ...) custom-call(bf16[1024,768]{1,0:T(8,128)(2,1)} %bitcast.102, ...), custom_call_target="tpu_custom_call" | custom-call | flops 13287555072 | bytes 27726336 | tf_op jit(solution)/shard_map/pallas_call | solution.py:527
  140.9 4.0 %convolution_convert_fusion.3 = bf16[768,768]{1,0:T(8,128)(2,1)} fusion(bf16[1024,768]{1,0:T(8,128)(2,1)S(1)} %copy-done.11, bf16[1024,768]{1,0:T(8,128)(2,1)} %get-tuple-element.50), kind=kOutput, calls=%fused_computation.6 | convolution fusion | flops 1208549376 | bytes 4325376 | tf_op jit(solution)/shard_map/dot_general | solution.py:637
  145.1 2.5 copy.37
  147.6 4.1 %convolution_convert_fusion.2 = bf16[4,4,72,768]{3,2,1,0:T(8,128)(2,1)S(1)} fusion(bf16[4,4,72,1024]{3,2,1,0:T(8,128)(2,1)} %bitcast.66, bf16[1,1024,768]{2,1,0:T(8,128)(2,1)} %param.17), kind=kOutput, calls=%fused_computation.3 | convolution fusion | flops 1812824064 | bytes 5701632 | tf_op jit(solution)/shard_map/dot_general | solution.py:641
  151.8 1.4 pad_maximum_fusion
  153.2 0.7 copy-done.13
  153.9 7.7 %convolution_convert_fusion.1 = bf16[768,2304]{1,0:T(8,128)(2,1)} fusion(bf16[1024,768]{1,0:T(8,128)(2,1)S(1)} %copy-done.13, bf16[1024,2304]{1,0:T(8,128)(2,1)} %get-tuple-element.47), kind=kOutput, calls=%fused_computation.1 | convolution fusion | flops 3625648128 | bytes 9830400 | tf_op jit(solution)/shard_map/dot_general | solution.py:637
  161.5 85.0 %shard_map.156 = (bf16[2,2,48,2304]{3,2,1,0:T(8,128)(2,1)}, bf16[2,2,80,768]{3,2,1,0:T(8,128)(2,1)}, bf16[2,2,48,768]{3,2,1,0:T(8,128)(2,1)}, bf16[1024,768]{1,0:T(8,128)(2,1)}, f32[1152,1536]{1,0:T(8,128)}) custom-call(bf16[4,2,2,48,2304]{4,3,2,1,0:T(8,128)(2,1)} %bitcast.64, bf16[4,2,2,80,768]{4,3,2,1,0:T(8,128)(2,1)} %bitcast.62, ...), custom_call_target="tpu_custom_call" | custom-call | tf_op jit(solution)/shard_map/pallas_call | solution.py:272
  246.6 0.8 fusion.14
  247.4 1.0 slice.104
  249.1 1.0 bitcast_convert_fusion.1
  250.1 1.4 bitcast_convert_fusion
  251.5 3.5 convert.36
  255.0 1.3 collective-permute-start.3
  256.3 3.0 collective-permute-start.2
  259.3 0.9 bitcast_convert_fusion.2
  261.1 7.8 %shard_map.157.d_qkv_ref = bf16[1024,2304]{1,0:T(8,128)(2,1)} custom-call(bf16[1024,768]{1,0:T(8,128)(2,1)} %get-tuple-element.53.d_q_ref, f32[1152,1536]{1,0:T(8,128)} %get-tuple-element.54.d_kv_ref, bf16[64,1536]{1,0:T(8,128)(2,1)} %copy-done.8, bf16[64,1536]{1,0:T(8,128)(2,1)} %copy-done.7, f32[1024,128]{1,0:T(8,128)} %get-tuple-element.71.cos_ref.refs_7_, ...), custom_call_target="tpu_custom_call" | custom-call | flops 6291456 | bytes 14811136 | tf_op jit(solution)/shard_map/pallas_call | solution.py:527
  268.9 6.4 %convolution_convert_fusion = bf16[768,2304]{1,0:T(8,128)(2,1)S(1)} fusion(bf16[1024,768]{1,0:T(8,128)(2,1)S(1)} %copy-done.12, bf16[1024,2304]{1,0:T(8,128)(2,1)} %shard_map.157.d_qkv_ref), kind=kOutput, calls=%fused_computation | convolution fusion | flops 3625648128 | bytes 9830400 | tf_op jit(solution)/shard_map/dot_general | solution.py:637
  275.4 1.7 slice.101
  277.1 0.7 copy-done
  277.8 10.4 %shard_map.158 = (f32[1024,768]{1,0:T(8,128)}, f32[1,768]{1,0:T(1,128)}) custom-call(bf16[1024,768]{1,0:T(8,128)(2,1)} %bitcast.103, bf16[1,768]{1,0:T(2,128)(2,1)} %reshape_squeeze.8.gain_ref, bf16[1024,2304]{1,0:T(8,128)(2,1)} %shard_map.157.d_qkv_ref, bf16[768,2304]{1,0:T(8,128)(2,1)} %bitcast.98, f32[1024,768]{1,0:T(8,128)} %get-tuple-element.55.d_resid_ref), custom_call_target="tpu_custom_call" | custom-call | flops 3623878656 | bytes 16126464 | tf_op jit(solution)/shard_map/pallas_call | solution.py:527
  288.2 0.7 convert_reduce_fusion
  289.1 1.3 pad_maximum_fusion.1.refs_1_
  290.4 54.9 %shard_map.159 = (bf16[2,2,48,1536]{3,2,1,0:T(8,128)(2,1)}, bf16[2,2,64,768]{3,2,1,0:T(8,128)(2,1)}) custom-call(bf16[4,2,2,48,1536]{4,3,2,1,0:T(8,128)(2,1)} %bitcast.61, bf16[4,2,2,64,768]{4,3,2,1,0:T(8,128)(2,1)} %pad_maximum_fusion.1.refs_1_), custom_call_target="tpu_custom_call" | custom-call | tf_op jit(solution)/shard_map/pallas_call | solution.py:272
  345.3 0.7 fusion.15
  346.0 1.0 slice.103
  347.7 2.4 maximum_convert_fusion
  (49 shorter events, 4.0 us)
Async XLA Ops:
  75.4 15.1 %copy-start.9 = (s32[1,1024]{1,0:T(1,128)S(1)}, s32[1,1024]{1,0:T(1,128)}, u32[]{:S(2)}) copy-start(s32[1,1024]{1,0:T(1,128)} %param.10) | copy-start | bytes 12292
  75.4 15.1 %copy-start.4 = (bf16[4,2,2,80,768]{4,3,2,1,0:T(8,128)(2,1)S(1)}, bf16[4,2,2,80,768]{4,3,2,1,0:T(8,128)(2,1)}, u32[]{:S(2)}) copy-start(bf16[4,2,2,80,768]{4,3,2,1,0:T(8,128)(2,1)} %get-tuple-element.36) | copy-start | bytes 5898244
  86.2 12.3 %collective-permute-start.1 = (bf16[64,1536]{1,0:T(8,128)(2,1)}, bf16[64,1536]{1,0:T(8,128)(2,1)S(1)}, u32[]{:S(2)}, u32[]{:S(2)}) collective-permute-start(bf16[64,1536]{1,0:T(8,128)(2,1)} %get-tuple-element.68), channel_id=1, source_target_pairs={{4,0},{8,4},{12,8},{16,12},{20,16},{24,20},{28,24},{5,1},{9,5},{13... | collective-permute-start | bytes 589832 | tf_op jit(solution)/shard_map/ppermute | solution.py:295
  87.4 10.8 %collective-permute-start = (bf16[64,1536]{1,0:T(8,128)(2,1)}, bf16[64,1536]{1,0:T(8,128)(2,1)S(1)}, u32[]{:S(2)}, u32[]{:S(2)}) collective-permute-start(bf16[64,1536]{1,0:T(8,128)(2,1)} %get-tuple-element.69), channel_id=1, source_target_pairs={{0,4},{4,8},{8,12},{12,16},{16,20},{20,24},{24,28},{1,5},{5,9},{9,... | collective-permute-start | bytes 589832 | tf_op jit(solution)/shard_map/ppermute | solution.py:295
  90.5 7.7 %copy-start.1 = (bf16[1024,1536]{1,0:T(8,128)(2,1)S(1)}, bf16[1024,1536]{1,0:T(8,128)(2,1)}, u32[]{:S(2)}) copy-start(bf16[1024,1536]{1,0:T(8,128)(2,1)} %get-tuple-element.39) | copy-start | bytes 9437188
  98.5 1.8 copy-start.2
  114.2 26.7 %copy-start.11 = (bf16[1024,768]{1,0:T(8,128)(2,1)S(1)}, bf16[1024,768]{1,0:T(8,128)(2,1)}, u32[]{:S(2)}) copy-start(bf16[1024,768]{1,0:T(8,128)(2,1)} %get-tuple-element.42.context_ref) | copy-start | bytes 4718596
  140.9 4.0 %copy-start.10 = (f32[1,768]{1,0:T(1,128)S(1)}, f32[1,768]{1,0:T(1,128)}, u32[]{:S(2)}) copy-start(f32[1,768]{1,0:T(1,128)} %get-tuple-element.49) | copy-start | bytes 9220
  140.9 4.2 %copy-start.3 = (bf16[1024,1152]{1,0:T(8,128)(2,1)S(1)}, bf16[1024,1152]{1,0:T(8,128)(2,1)}, u32[]{:S(2)}) copy-start(bf16[1024,1152]{1,0:T(8,128)(2,1)} %get-tuple-element.48) | copy-start | bytes 7077892
  151.8 2.1 copy-start.13
  246.6 3.5 copy-start.5
  251.5 7.9 %copy-start.6 = (bf16[2,2,48,768]{3,2,1,0:T(8,128)(2,1)S(1)}, bf16[2,2,48,768]{3,2,1,0:T(8,128)(2,1)}, u32[]{:S(2)}) copy-start(bf16[2,2,48,768]{3,2,1,0:T(8,128)(2,1)} %get-tuple-element.61) | copy-start | bytes 884740
  255.0 5.2 %collective-permute-start.3 = (bf16[64,1536]{1,0:T(8,128)(2,1)S(1)}, bf16[64,1536]{1,0:T(8,128)(2,1)S(1)}, u32[]{:S(2)}, u32[]{:S(2)}) collective-permute-start(bf16[64,1536]{1,0:T(8,128)(2,1)S(1)} %get-tuple-element.66), channel_id=1, source_target_pairs={{4,0},{8,4},{12,8},{16,12},{20,16},{24,20},{28,24},{5,1},{9,5},{13... | collective-permute-start | bytes 589832 | tf_op jit(solution)/shard_map/ppermute | solution.py:295
  256.3 4.1 %collective-permute-start.2 = (bf16[64,1536]{1,0:T(8,128)(2,1)S(1)}, bf16[64,1536]{1,0:T(8,128)(2,1)S(1)}, u32[]{:S(2)}, u32[]{:S(2)}) collective-permute-start(bf16[64,1536]{1,0:T(8,128)(2,1)S(1)} %get-tuple-element.67), channel_id=1, source_target_pairs={{0,4},{4,8},{8,12},{12,16},{16,20},{20,24},{24,28},{1,5},{5,9},{9,... | collective-permute-start | bytes 589832 | tf_op jit(solution)/shard_map/ppermute | solution.py:295
  260.2 0.7 copy-start.7
  260.4 0.7 copy-start.8
  261.1 7.9 %copy-start.12 = (bf16[1024,768]{1,0:T(8,128)(2,1)S(1)}, bf16[1024,768]{1,0:T(8,128)(2,1)}, u32[]{:S(2)}) copy-start(bf16[1024,768]{1,0:T(8,128)(2,1)} %get-tuple-element.57) | copy-start | bytes 4718596
  275.3 2.5 copy-start
  277.8 11.3 %slice-start = ((bf16[768,2304]{1,0:T(8,128)(2,1)}), bf16[768,768]{1,0:T(8,128)(2,1)S(1)}, s32[]{:S(2)}) async-start(bf16[768,2304]{1,0:T(8,128)(2,1)} %copy-done), calls=%async_computation | async-start | bytes 2359296 | tf_op jit(solution)/shard_map/slice | solution.py:672
